TPU v7x, 256 devices: a whole 4x4x8 slice. The times are simulated.
256 devices in a mesh: dp: 32 (over z, x), tensor: 8 (over y, core).
Axes of the slice: x: 4, y: 4, z: 8, core: 2. Of those that a mesh axis runs over, the one named last changes fastest.
Arguments:
- tokens: bfloat16 [65536, 8192], P('dp', 'tensor'), may hold values from -6 to 6
- value_projection_weight: bfloat16 [8192, 1024], P('tensor'), may hold values from -0.0625 to 0.0625
- adapter_down_factors: bfloat16 [1024, 8192, 64], P('dp', 'tensor'), may hold values from -0.0625 to 0.0625
- adapter_up_factors: bfloat16 [1024, 64, 1024], P('dp', None, 'tensor'), may hold values from -0.75 to 0.75
- block_adapter_table: int32 [32, 16], P('dp'), may hold values from 0 to 1023, as said below
Outputs:
- values_out: bfloat16 [65536, 1024], P('dp', 'tensor')
Inputs may be any that keep to these rules, and one draw needn't show every extreme that they name: `block_adapter_table`: adapter a is owned by index a // 32 of dp. In each microbatch no dp index owns the adapters of more than 1 block, and each dp index that owns any of them owns exactly 1.
All inputs are finite; a program needn't handle non-finite values.
Results may differ from a plain program's by a relative error of at most 0.0039.
Values may be sent and summed in bfloat16 or wider, within the bound.
No kernel may reach another device: no remote copies, remote signals or barrier semaphores. Data moves between devices by JAX's collectives and lax.ppermute only.
A program may use at most 128 MiB of HBM per device.

v0:
```python
import jax
import jax.numpy as jnp
from jax import lax
from jax.sharding import PartitionSpec as P

BLOCK = 128


def slot_table(adapter_ids, adapter_per_device):
    owner_of = adapter_ids // adapter_per_device
    count = adapter_ids.shape[1]
    same = owner_of[:, :, None] == owner_of[:, None, :]
    earlier = lax.broadcasted_iota(jnp.int32, (count, count), 1) < lax.broadcasted_iota(
        jnp.int32, (count, count), 0
    )
    rank = jnp.sum((same & earlier[None, :, :]).astype(jnp.int32), axis=2)
    return (owner_of, rank)


def local(
    tokens, value_projection_weight, adapter_down_factors, adapter_up_factors, block_adapter_table
):
    groups = lax.axis_size("dp")
    device_index = lax.axis_index("dp")
    rows_dev, feat_dev = tokens.shape
    blocks = rows_dev // BLOCK
    capacity = max(1, 2 * blocks // groups)
    adapter_per_device = adapter_down_factors.shape[0]
    rank_dimension = adapter_down_factors.shape[2]
    value_per_device = adapter_up_factors.shape[2]
    slot_iota = jnp.arange(capacity, dtype=jnp.int32)
    all_ids = lax.all_gather(block_adapter_table, "dp", axis=0, tiled=True)
    owner_every_group, rank_all = slot_table(all_ids, adapter_per_device)
    matches = (owner_every_group == device_index)[:, None, :] & (
        rank_all[:, None, :] == slot_iota[None, :, None]
    )
    local_all = all_ids - device_index * adapter_per_device
    slot_position_index = jnp.sum(jnp.where(matches, local_all[:, None, :], 0), axis=2).reshape(-1)
    slot_valid_mask = jnp.any(matches, axis=2).reshape(-1).astype(jnp.bfloat16)
    owner_mine, rank_mine = slot_table(block_adapter_table, adapter_per_device)
    owner_mine = owner_mine[0]
    rank_mine = rank_mine[0]
    slot_mine = owner_mine * capacity + rank_mine
    token_blocks = tokens.reshape(blocks, BLOCK, feat_dev)
    up_factor_outgoing = (
        adapter_up_factors[slot_position_index] * slot_valid_mask[:, None, None]
    ).reshape(groups, capacity, rank_dimension, value_per_device)
    group_iota = jnp.arange(groups, dtype=jnp.int32)
    block_iota = jnp.arange(blocks, dtype=jnp.int32)
    wanted = (owner_mine[None, None, :] == group_iota[:, None, None]) & (
        rank_mine[None, None, :] == slot_iota[None, :, None]
    )
    source = jnp.sum(jnp.where(wanted, block_iota[None, None, :], 0), axis=2).reshape(-1)
    present = jnp.any(wanted, axis=2).reshape(-1).astype(jnp.bfloat16)
    send_rows = (token_blocks[source] * present[:, None, None]).reshape(
        groups, capacity, BLOCK, feat_dev
    )
    received = lax.all_to_all(send_rows, "dp", split_axis=0, concat_axis=0, tiled=True)
    down_factor_used = adapter_down_factors[slot_position_index]
    partial_value = jnp.einsum(
        "kbd,kdr->kbr",
        received.reshape(groups * capacity, BLOCK, feat_dev),
        down_factor_used,
        preferred_element_type=jnp.float32,
    )
    returned = lax.all_to_all(
        partial_value.reshape(groups, capacity, BLOCK, rank_dimension),
        "dp",
        split_axis=0,
        concat_axis=0,
        tiled=True,
    )
    down_projection_part = returned.reshape(groups * capacity, BLOCK, rank_dimension)[slot_mine]
    up_recv = lax.all_to_all(up_factor_outgoing, "dp", split_axis=0, concat_axis=0, tiled=True)
    base_part = jnp.dot(tokens, value_projection_weight, preferred_element_type=jnp.float32)
    base = lax.psum_scatter(base_part, "tensor", scatter_dimension=1, tiled=True)
    low_rank_output = lax.psum(down_projection_part, "tensor").astype(jnp.bfloat16)
    up_blocks = up_recv.reshape(groups * capacity, rank_dimension, value_per_device)[slot_mine]
    delta = jnp.einsum(
        "kbr,krv->kbv", low_rank_output, up_blocks, preferred_element_type=jnp.float32
    )
    return (base + delta.reshape(rows_dev, value_per_device)).astype(jnp.bfloat16)


def solution(mesh):
    placed = (
        P("dp", "tensor"),
        P("tensor", None),
        P("dp", "tensor", None),
        P("dp", None, "tensor"),
        P("dp", None),
    )
    return jax.shard_map(
        local, mesh=mesh, in_specs=placed, out_specs=P("dp", "tensor"), check_vma=False
    )
```

profile of v0, /device:TPU:1, one launch (start us, length us, event | category | flops | bytes accessed | tf_op | source)
XLA Modules:
  0.0 349.6 jit_solution(4953530165614802863)
XLA Ops:
  6.5 0.0 copy-start
  6.5 0.8 fusion.27
  7.3 0.2 convert_reduce_fusion.1
  7.5 0.1 select_reduce_fusion
  7.6 0.1 fusion.13
  7.8 7.1 %gather_fusion = bf16[32,128,1024]{2,1,0:T(8,128)(2,1)} fusion(bf16[16,128,1024]{2,1,0:T(8,128)(2,1)} %bitcast.68, s32[1024]{0:T(1024)S(1)} %pad_clamp_fusion.2), kind=kCustom, calls=%fused_computation | custom fusion | bytes 16777344 | tf_op jit(solution)/shard_map/gather | solution.py:55
  14.9 7.2 %bitcast_multiply_fusion = bf16[32,1,128,1024]{3,2,1,0:T(8,128)(2,1)} fusion(bf16[32,128,1024]{2,1,0:T(8,128)(2,1)} %gather_fusion, bf16[32]{0:T(256)(128)(2,1)S(1)} %convert_element_type.35), kind=kLoop, calls=%fused_computation.7 | loop fusion | flops 4194304 | bytes 16777280 | tf_op jit(solution)/shard_map/mul | solution.py:55
  22.1 12.0 %all-to-all-start = ((bf16[32,1,128,1024]{3,2,1,0:T(8,128)(2,1)}), bf16[32,1,128,1024]{3,2,1,0:T(8,128)(2,1)}, u32[]{:S(2)}, u32[]{:S(2)}) async-start(bf16[32,1,128,1024]{3,2,1,0:T(8,128)(2,1)} %bitcast_multiply_fusion), calls=%async_computation.1 | async-start | bytes 16777216 | tf_op jit(solution)/shard_map/all_to_all | solution.py:58
  34.1 0.0 reduce-scatter.2.cloned.1.call-start
  34.2 0.0 copy-done
  34.2 9.0 %fusion.20 = f32[2048,1024]{1,0:T(8,128)} fusion(bf16[2048,1024]{1,0:T(8,128)(2,1)} %param.5, bf16[1024,1024]{1,0:T(8,128)(2,1)S(1)} %copy-done), kind=kOutput, calls=%fused_computation.52 | convolution fusion | flops 4294967296 | bytes 14680064 | tf_op jit(solution)/shard_map/dot_general | solution.py:75
  43.2 0.0 copy-start.4
  43.2 0.0 copy-start.3
  43.2 0.0 reduce-scatter.2.cloned.1.call-update
  43.2 0.6 copy-done.4
  43.8 207.9 %all-gather = s32[32,1,16]{2,1,0:T(1,128)S(1)} all-gather(s32[1,1,16]{2,1,0:T(1,128)S(1)} %bitcast.71), channel_id=1, replica_groups=mesh['dp'=32,'tensor'=8] {'dp'}, dimensions={0}, use_global_device_ids=true | all-gather | bytes 2112 | tf_op jit(solution)/shard_map/all_gather | solution.py:32
  251.7 0.1 copy.7
  251.8 0.1 convert_reduce_fusion
  252.0 0.0 copy-done.3
  252.0 0.6 gather_fusion.3
  252.7 0.9 bitcast_multiply_fusion.1
  253.6 0.0 all-to-all-done
  253.6 4.7 %all-to-all-start.2 = ((bf16[32,1,64,128]{3,2,1,0:T(8,128)(2,1)}), bf16[32,1,64,128]{3,2,1,0:T(8,128)(2,1)S(1)}, u32[]{:S(2)}, u32[]{:S(2)}) async-start(bf16[32,1,64,128]{3,2,1,0:T(8,128)(2,1)} %bitcast_multiply_fusion.1), calls=%async_computation.3 | async-start | bytes 1048576 | tf_op jit(solution)/shard_map/all_to_all | solution.py:74
  258.3 4.9 %gather_fusion.1 = bf16[32,1024,64]{1,2,0:T(8,128)(2,1)} fusion(bf16[32,1024,64]{1,2,0:T(8,128)(2,1)} %param.7, s32[1024]{0:T(1024)S(1)} %pad_clamp_fusion.1), kind=kCustom, calls=%fused_computation.1 | custom fusion | bytes 8388736 | tf_op jit(solution)/shard_map/gather | solution.py:59
  263.2 8.5 %fusion.2 = f32[32,1,128,64]{2,3,1,0:T(8,128)} fusion(bf16[32,1024,64]{1,2,0:T(8,128)(2,1)} %gather_fusion.1, bf16[32,1,128,1024]{3,2,1,0:T(8,128)(2,1)} %all-to-all-done), kind=kOutput, calls=%fused_computation.8 | convolution fusion | flops 536870912 | bytes 13631488 | tf_op jit(solution)/shard_map/kbd,kdr->kbr/dot_general | solution.py:60
  271.7 0.0 all-to-all-done.2
  271.7 0.0 copy-start.2
  271.7 0.8 copy-done.2
  272.5 9.2 %all-to-all-start.1 = ((f32[32,1,128,64]{2,3,1,0:T(8,128)}), f32[32,1,128,64]{2,3,1,0:T(8,128)S(1)}, u32[]{:S(2)}, u32[]{:S(2)}) async-start(f32[32,1,128,64]{2,3,1,0:T(8,128)} %fusion.2), calls=%async_computation.2 | async-start | bytes 2097152 | tf_op jit(solution)/shard_map/all_to_all | solution.py:66
  281.8 2.3 gather_fusion.4
  284.1 15.6 %all-to-all-done.1 = f32[32,1,128,64]{2,3,1,0:T(8,128)S(1)} async-done(((f32[32,1,128,64]{2,3,1,0:T(8,128)}), f32[32,1,128,64]{2,3,1,0:T(8,128)S(1)}, u32[]{:S(2)}, u32[]{:S(2)}) %all-to-all-start.1) | async-done | bytes 1048608 | tf_op jit(solution)/shard_map/all_to_all | solution.py:66
  299.8 0.0 copy-start.1
  299.8 1.1 copy-done.1
  300.8 1.8 gather_fusion.2
  302.6 36.7 %all-reduce.1 = bf16[16,128,64]{1,2,0:T(8,128)(2,1)S(1)} all-reduce(f32[16,128,64]{1,2,0:T(8,128)S(1)} %gather_fusion.2), channel_id=1, replica_groups=mesh['dp'=32,'tensor'=8] {'tensor'}, use_global_device_ids=true, to_apply=%region_6.7 | all-reduce | flops 131072 | bytes 786432 | tf_op jit(solution)/shard_map/psum | solution.py:77
  339.3 1.3 fusion.21
  340.7 0.0 reduce-scatter.2.cloned.1.call-done
  340.7 2.1 fusion.5
  (13 shorter events, 0.1 us)
Async XLA Ops:
  6.5 27.6 %copy-start = (bf16[1024,1024]{1,0:T(8,128)(2,1)S(1)}, bf16[1024,1024]{1,0:T(8,128)(2,1)}, u32[]{:S(2)}) copy-start(bf16[1024,1024]{1,0:T(8,128)(2,1)} %param.6) | copy-start | bytes 6291460
  22.1 231.5 %all-to-all-start = ((bf16[32,1,128,1024]{3,2,1,0:T(8,128)(2,1)}), bf16[32,1,128,1024]{3,2,1,0:T(8,128)(2,1)}, u32[]{:S(2)}, u32[]{:S(2)}) async-start(bf16[32,1,128,1024]{3,2,1,0:T(8,128)(2,1)} %bitcast_multiply_fusion), calls=%async_computation.1 | async-start | bytes 16777216 | tf_op jit(solution)/shard_map/all_to_all | solution.py:58
  34.1 306.6 %reduce-scatter.2.cloned.1.call-start = ((), (), s32[]{:S(2)}) async-start(), calls=%async_computation.4 | async-start | bytes 9437184 | tf_op jit(solution)/shard_map/reduce_scatter | solution.py:76
  43.2 0.7 copy-start.4
  43.2 208.8 %copy-start.3 = (bf16[32,64,128]{2,1,0:T(8,128)(2,1)S(1)}, bf16[32,64,128]{2,1,0:T(8,128)(2,1)}, u32[]{:S(2)}) copy-start(bf16[32,64,128]{2,1,0:T(8,128)(2,1)} %param.8) | copy-start | bytes 1572868
  253.6 18.2 %all-to-all-start.2 = ((bf16[32,1,64,128]{3,2,1,0:T(8,128)(2,1)}), bf16[32,1,64,128]{3,2,1,0:T(8,128)(2,1)S(1)}, u32[]{:S(2)}, u32[]{:S(2)}) async-start(bf16[32,1,64,128]{3,2,1,0:T(8,128)(2,1)} %bitcast_multiply_fusion.1), calls=%async_computation.3 | async-start | bytes 1048576 | tf_op jit(solution)/shard_map/all_to_all | solution.py:74
  271.7 0.8 copy-start.2
  272.5 27.2 %all-to-all-start.1 = ((f32[32,1,128,64]{2,3,1,0:T(8,128)}), f32[32,1,128,64]{2,3,1,0:T(8,128)S(1)}, u32[]{:S(2)}, u32[]{:S(2)}) async-start(f32[32,1,128,64]{2,3,1,0:T(8,128)} %fusion.2), calls=%async_computation.2 | async-start | bytes 2097152 | tf_op jit(solution)/shard_map/all_to_all | solution.py:66
  299.8 1.1 copy-start.1
Sparse Core Ops, SparseCore 0:
  43.3 56.0 reduce-scatter.1
where the time goes:
time: 353 us; the launch traced here: 350 us
  blocking collectives  245 us (69%)
  starting transfers between devices  26 us (7%)
  local copies, waits for them, and re-layouts  19.4 us (5%)
  matrix products  18.8 us (5%)
  waiting for transfers between devices  15.7 us (4%)
  between operations  13.5 us (4%)
  other arithmetic  11.7 us (3%)
    all_gather x1, blocking collectives, local(): all_ids = lax.all_gather(block_adapter_table, 'dp', axis=0, tiled=True)  208 us
    psum x1, blocking collectives, local(): lax.psum(down_projection_part, 'tensor').astype(jnp.bfloat16)  36.7 us
    all_to_all x1, waiting for transfers between devices, local(): lax.all_to_all(partial_value.reshape(groups, capacity, BLOCK, rank_dimens...  15.6 us
    all_to_all x1, starting transfers between devices, local(): lax.all_to_all(send_rows, 'dp', split_axis=0, concat_axis=0, tiled=True)  12 us
    all_to_all x1, starting transfers between devices, local(): lax.all_to_all(partial_value.reshape(groups, capacity, BLOCK, rank_dimens...  9.22 us
    dot_general x1, matrix products, local(): jnp.dot(tokens, value_projection_weight, preferred_element_type=jnp.float32)  9 us
    dot_general x1, matrix products, local(): jnp.einsum('kbd,kdr->kbr', received.reshape(groups * capacity, BLOCK, fea...  8.54 us
    mul x1, other arithmetic, local(): token_blocks[source] * present[:, None, None]  7.21 us
  transfers between devices with their start and end apart: 4, of which 1 were waited for; matrix products, arithmetic and copies ran while one was open for 9% of the time, Pallas kernels for 0%

commit v1 on v0

v1 whole, which is shorter than its diff:
```python
import jax
import jax.numpy as jnp
from jax import lax
from jax.experimental import pallas as pl
from jax.experimental.pallas import tpu as pltpu
from jax.sharding import PartitionSpec as P

BLOCK = 128


def pick_kernel(ids_ref, down_ref, up_ref, out_ref, buf, insem, outsem):
    slots, rank, width = out_ref.shape
    feat = down_ref.shape[2]
    loads = []
    stores = []
    for s in range(slots):
        i = ids_ref[s, 0]
        loads.append(
            (
                pltpu.make_async_copy(
                    down_ref.at[i], buf.at[s, :, pl.ds(0, feat)], insem.at[0, s]
                ),
                pltpu.make_async_copy(
                    up_ref.at[i], buf.at[s, :, pl.ds(feat, width - feat)], insem.at[1, s]
                ),
            )
        )
        stores.append(pltpu.make_async_copy(buf.at[s], out_ref.at[s], outsem.at[s]))
    for pair in loads:
        for c in pair:
            c.start()
    for pair, store in zip(loads, stores):
        for c in pair:
            c.wait()
        store.start()
    for store in stores:
        store.wait()


def pick(ids, down_t, up):
    slots = ids.shape[0]
    _, rank, feat = down_t.shape
    width = feat + up.shape[2]
    return pl.pallas_call(
        pick_kernel,
        out_shape=jax.ShapeDtypeStruct((slots, rank, width), down_t.dtype),
        in_specs=[
            pl.BlockSpec(memory_space=pltpu.SMEM),
            pl.BlockSpec(memory_space=pltpu.HBM),
            pl.BlockSpec(memory_space=pltpu.HBM),
        ],
        out_specs=pl.BlockSpec(memory_space=pltpu.HBM),
        scratch_shapes=[
            pltpu.VMEM((slots, rank, width), down_t.dtype),
            pltpu.SemaphoreType.DMA((2, slots)),
            pltpu.SemaphoreType.DMA((slots,)),
        ],
        compiler_params=pltpu.CompilerParams(vmem_limit_bytes=62 * 1024 * 1024),
    )(ids, down_t, up)


def down_kernel(owner_ref, tok_ref, recv_ref, part_ref, up_ref, tok, fac, tsem, fsem):
    blocks, rows, feat = tok.shape
    tcopies = []
    fcopies = []
    for b in range(blocks):
        fcopies.append(
            pltpu.make_async_copy(recv_ref.at[owner_ref[b]], fac.at[b], fsem.at[b])
        )
        tcopies.append(pltpu.make_async_copy(tok_ref.at[b], tok.at[b], tsem.at[b]))
    for b in range(blocks):
        fcopies[b].start()
        tcopies[b].start()
    for b in range(blocks):
        fcopies[b].wait()
        tcopies[b].wait()
        part_ref[b] = lax.dot_general(
            fac[b, :, :feat],
            tok[b],
            (((1,), (1,)), ((), ())),
            preferred_element_type=jnp.float32,
        ).astype(jnp.bfloat16)
        up_ref[b] = fac[b, :, feat:]


def down_products(owner, token_blocks, recv):
    blocks, rows, feat = token_blocks.shape
    _, rank, width = recv.shape
    vmem = pl.BlockSpec(memory_space=pltpu.VMEM)
    hbm = pl.BlockSpec(memory_space=pltpu.HBM)
    return pl.pallas_call(
        down_kernel,
        out_shape=(
            jax.ShapeDtypeStruct((blocks, rank, rows), jnp.bfloat16),
            jax.ShapeDtypeStruct((blocks, rank, width - feat), jnp.bfloat16),
        ),
        in_specs=[pl.BlockSpec(memory_space=pltpu.SMEM), hbm, hbm],
        out_specs=(vmem, vmem),
        scratch_shapes=[
            pltpu.VMEM((blocks, rows, feat), jnp.bfloat16),
            pltpu.VMEM((blocks, rank, width), jnp.bfloat16),
            pltpu.SemaphoreType.DMA((blocks,)),
            pltpu.SemaphoreType.DMA((blocks,)),
        ],
        compiler_params=pltpu.CompilerParams(vmem_limit_bytes=62 * 1024 * 1024),
    )(owner, token_blocks, recv)


def final_kernel(parts_ref, up_ref, base_ref, out_ref, parts, base, psem, bsem):
    blocks, shares, rank, rows = parts.shape
    pcopies = []
    bcopies = []
    for b in range(blocks):
        span = pl.ds(b * rows, rows)
        pcopies.append(pltpu.make_async_copy(parts_ref.at[:, b], parts.at[b], psem.at[b]))
        bcopies.append(
            pltpu.make_async_copy(base_ref.at[span, :], base.at[span, :], bsem.at[b])
        )
    for b in range(blocks):
        pcopies[b].start()
        bcopies[b].start()
    for b in range(blocks):
        span = pl.ds(b * rows, rows)
        pcopies[b].wait()
        total = parts[b, 0].astype(jnp.float32)
        for s in range(1, shares):
            total += parts[b, s].astype(jnp.float32)
        delta = lax.dot_general(
            total.astype(jnp.bfloat16),
            up_ref[b],
            (((0,), (0,)), ((), ())),
            preferred_element_type=jnp.float32,
        )
        bcopies[b].wait()
        out_ref[span, :] = (base[span, :] + delta).astype(jnp.bfloat16)


def finish(parts, up_blocks, base):
    shares, blocks, rank, rows = parts.shape
    vmem = pl.BlockSpec(memory_space=pltpu.VMEM)
    hbm = pl.BlockSpec(memory_space=pltpu.HBM)
    return pl.pallas_call(
        final_kernel,
        out_shape=jax.ShapeDtypeStruct(base.shape, jnp.bfloat16),
        in_specs=[hbm, vmem, hbm],
        out_specs=vmem,
        scratch_shapes=[
            pltpu.VMEM((blocks, shares, rank, rows), parts.dtype),
            pltpu.VMEM(base.shape, base.dtype),
            pltpu.SemaphoreType.DMA((blocks,)),
            pltpu.SemaphoreType.DMA((blocks,)),
        ],
        compiler_params=pltpu.CompilerParams(vmem_limit_bytes=62 * 1024 * 1024),
    )(parts, up_blocks, base)


def local(
    tokens, value_projection_weight, adapter_down_factors, adapter_up_factors, block_adapter_table
):
    groups = lax.axis_size("dp")
    rows_dev, feat_dev = tokens.shape
    blocks = rows_dev // BLOCK
    adapter_per_device = adapter_down_factors.shape[0]
    ids = block_adapter_table[0]
    owner = ids // adapter_per_device
    hit = owner[None, :] == jnp.arange(groups, dtype=jnp.int32)[:, None]
    asked = jnp.sum(jnp.where(hit, (ids - owner * adapter_per_device)[None, :], 0), axis=1)
    wanted = lax.all_to_all(asked[:, None], "dp", split_axis=0, concat_axis=0, tiled=True)
    outgoing = pick(wanted, jnp.swapaxes(adapter_down_factors, 1, 2), adapter_up_factors)
    base_part = jnp.dot(tokens, value_projection_weight, preferred_element_type=jnp.float32)
    outgoing, base_part = lax.optimization_barrier((outgoing, base_part))
    received = lax.all_to_all(outgoing, "dp", split_axis=0, concat_axis=0, tiled=True)
    base = lax.psum_scatter(base_part, "tensor", scatter_dimension=1, tiled=True)
    received, base = lax.optimization_barrier((received, base))
    part, up_blocks = down_products(owner, tokens.reshape(blocks, BLOCK, feat_dev), received)
    parts = lax.all_gather(part, "tensor", axis=0)
    return finish(parts, up_blocks, base)


def solution(mesh):
    placed = (
        P("dp", "tensor"),
        P("tensor", None),
        P("dp", "tensor", None),
        P("dp", None, "tensor"),
        P("dp", None),
    )
    return jax.shard_map(
        local, mesh=mesh, in_specs=placed, out_specs=P("dp", "tensor"), check_vma=False
    )
```

time: 353 us -> 202 us (0.57)
  blocking collectives: 245 us -> 0 us
  waiting for transfers between devices: 15.7 us -> 132 us
  Pallas kernels: 0 us -> 19.6 us
  local copies, waits for them, and re-layouts: 19.4 us -> 1.31 us
  other arithmetic: 11.7 us -> 1.3 us
  matrix products: 18.8 us -> 10.6 us
    all_gather x1 -> x0, blocking collectives: 208 us -> none  [local(): all_ids = lax.all_gather(block_adapter_table, 'dp', axis=0, tiled=True)]
    all_to_all x3 -> x2, waiting for transfers between devices: 15.6 us -> 103 us  [the longest x1 103 us: local(): lax.all_to_all(outgoing, 'dp', split_axis=0, concat_axis=0, tiled=True)]
    psum x1 -> x0, blocking collectives: 36.7 us -> none  [local(): lax.psum(down_projection_part, 'tensor').astype(jnp.bfloat16)]
    all_gather x0 -> x1, waiting for transfers between devices: none -> 29.4 us  [local(): parts = lax.all_gather(part, 'tensor', axis=0)]
    pallas_call x0 -> x3, Pallas kernels: none -> 19.6 us  [the longest x1 7.09 us: down_products(): pl.pallas_call(down_kernel, out_shape=(jax.ShapeDtypeStruct((blocks, rank...]
    gather x5 -> x0, local copies, waits for them, and re-layouts: 16.8 us -> none  [the longest x1 7.13 us: local(): token_blocks[source] * present[:, None, None]]
    dot_general x2 -> x0, matrix products: 9.84 us -> none  [the longest x1 8.54 us: local(): jnp.einsum('kbd,kdr->kbr', received.reshape(groups * capacity, BLOCK, fea...]
    mul x2 -> x0, other arithmetic: 8.11 us -> none  [the longest x1 7.21 us: local(): token_blocks[source] * present[:, None, None]]
  transfers between devices with their start and end apart: 4 -> 4, of which waited for: 1 -> 2; matrix products, arithmetic and copies ran while one was open for 9% -> 6% of each run, Pallas kernels for 0% -> 0%
where the time goes in v1:
time: 202 us
  waiting for transfers between devices  132 us (65%)
  starting transfers between devices  23.6 us (12%)
  Pallas kernels  19.6 us (10%)
  between operations  13.5 us (7%)
  matrix products  10.6 us (5%)
    all_to_all x1, waiting for transfers between devices, local(): lax.all_to_all(outgoing, 'dp', split_axis=0, concat_axis=0, tiled=True)  103 us
    all_gather x1, waiting for transfers between devices, local(): parts = lax.all_gather(part, 'tensor', axis=0)  29.4 us
    all_to_all x1, starting transfers between devices, local(): lax.all_to_all(asked[:, None], 'dp', split_axis=0, concat_axis=0, tiled=T...  11.9 us
    all_to_all x1, starting transfers between devices, local(): lax.all_to_all(outgoing, 'dp', split_axis=0, concat_axis=0, tiled=True)  11.6 us
    dot_general x1, matrix products, local(): jnp.dot(tokens, value_projection_weight, preferred_element_type=jnp.float32)  10.6 us
    pallas_call x1, Pallas kernels, down_products(): pl.pallas_call(down_kernel, out_shape=(jax.ShapeDtypeStruct((blocks, rank...  7.09 us
    pallas_call x1, Pallas kernels, pick(): pl.pallas_call(pick_kernel, out_shape=jax.ShapeDtypeStruct((slots, rank,...  6.32 us
    pallas_call x1, Pallas kernels, finish(): pl.pallas_call(final_kernel, out_shape=jax.ShapeDtypeStruct(base.shape, j...  6.22 us
  transfers between devices with their start and end apart: 4, of which 2 were waited for; matrix products, arithmetic and copies ran while one was open for 6% of the time, Pallas kernels for 0%

profile of v1, /device:TPU:1, one launch (start us, length us, event | category | flops | bytes accessed | tf_op | source)
XLA Modules:
  0.0 202.1 jit_solution(5395166609916758961)
XLA Ops:
  6.5 0.7 subtract_bitcast_fusion
  7.2 0.1 select_reduce_fusion
  7.3 0.7 copy.11
  8.0 11.9 %all-to-all-start = ((s32[32,1,1]{2,1,0:T(1,128)}), s32[32,1,1]{2,1,0:T(1,128)S(1)}, u32[]{:S(2)}, u32[]{:S(2)}) async-start(s32[32,1,1]{2,1,0:T(1,128)} %copy.11), calls=%async_computation | async-start | bytes 32768 | tf_op jit(solution)/shard_map/all_to_all | solution.py:168
  19.9 0.0 reduce-scatter.2.cloned.1.call-start
  19.9 10.6 %fusion = f32[2048,1024]{1,0:T(8,128)} fusion(bf16[2048,1024]{1,0:T(8,128)(2,1)} %param.5, bf16[1024,1024]{1,0:T(8,128)(2,1)} %param.6), kind=kOutput, calls=%fused_computation.12 | convolution fusion | flops 4294967296 | bytes 14680064 | tf_op jit(solution)/shard_map/dot_general | solution.py:170
  30.5 0.0 all-to-all-done
  30.5 0.0 copy-start
  30.5 0.6 copy-done
  31.1 6.3 %shard_map.55 = bf16[32,64,1152]{2,1,0:T(8,128)(2,1)} custom-call(s32[32,1]{1,0:T(8,128)} %bitcast.21, bf16[32,64,1024]{2,1,0:T(8,128)(2,1)} %bitcast.18, bf16[32,64,128]{2,1,0:T(8,128)(2,1)} %up_ref.1), custom_call_target="tpu_custom_call" | custom-call | tf_op jit(solution)/shard_map/pallas_call | solution.py:44
  37.5 0.0 reduce-scatter.2.cloned.1.call-update
  37.5 0.0 copy-start.1
  37.5 11.6 %all-to-all-start.1 = ((bf16[32,64,1152]{2,1,0:T(8,128)(2,1)}), bf16[32,64,1152]{2,1,0:T(8,128)(2,1)}, u32[]{:S(2)}, u32[]{:S(2)}) async-start(bf16[32,64,1152]{2,1,0:T(8,128)(2,1)} %shard_map.55), calls=%async_computation.1 | async-start | bytes 9437184 | tf_op jit(solution)/shard_map/all_to_all | solution.py:172
  49.1 0.0 all-gather.3.cloned.1.call-start
  49.2 0.0 copy-done.1
  49.2 0.5 and_select_fusion.1.owner_ref
  49.7 102.7 %all-to-all-done.1.recv_ref = bf16[32,64,1152]{2,1,0:T(8,128)(2,1)} async-done(((bf16[32,64,1152]{2,1,0:T(8,128)(2,1)}), bf16[32,64,1152]{2,1,0:T(8,128)(2,1)}, u32[]{:S(2)}, u32[]{:S(2)}) %all-to-all-start.1) | async-done | bytes 4718624 | tf_op jit(solution)/shard_map/all_to_all | solution.py:172
  152.5 0.0 reduce-scatter.2.cloned.1.call-done.base_ref
  152.5 7.1 %shard_map.56 = (bf16[16,64,128]{2,1,0:T(8,128)(2,1)}, bf16[16,64,128]{2,1,0:T(8,128)(2,1)}) custom-call(s32[16]{0:T(128)} %and_select_fusion.1.owner_ref, bf16[16,128,1024]{2,1,0:T(8,128)(2,1)} %bitcast.19, bf16[32,64,1152]{2,1,0:T(8,128)(2,1)} %all-to-all-done.1.recv_ref), custom_call_target="tpu_custom_call" | custom-call | tf_op jit(solution)/shard_map/pallas_call | solution.py:91
  159.6 0.0 all-gather.3.cloned.1.call-update
  159.6 29.4 %all-gather.3.cloned.1.call-done = bf16[128,64,128]{2,1,0:T(8,128)(2,1)} async-done(((bf16[16,64,128]{2,1,0:T(8,128)(2,1)}), bf16[128,64,128]{2,1,0:T(8,128)(2,1)}) %all-gather.3.cloned.1.call-update) | async-done | bytes 2097168 | tf_op jit(solution)/shard_map/all_gather | solution.py:176
  189.0 6.2 %shard_map.57 = bf16[2048,128]{1,0:T(8,128)(2,1)} custom-call(bf16[8,16,64,128]{3,2,1,0:T(8,128)(2,1)} %bitcast.20, bf16[16,64,128]{2,1,0:T(8,128)(2,1)} %get-tuple-element.15.up_ref, f32[2048,128]{1,0:T(8,128)} %reduce-scatter.2.cloned.1.call-done.base_ref), custom_call_target="tpu_custom_call" | custom-call | tf_op jit(solution)/shard_map/pallas_call | solution.py:142
Async XLA Ops:
  8.0 22.6 %all-to-all-start = ((s32[32,1,1]{2,1,0:T(1,128)}), s32[32,1,1]{2,1,0:T(1,128)S(1)}, u32[]{:S(2)}, u32[]{:S(2)}) async-start(s32[32,1,1]{2,1,0:T(1,128)} %copy.11), calls=%async_computation | async-start | bytes 32768 | tf_op jit(solution)/shard_map/all_to_all | solution.py:168
  19.9 132.6 %reduce-scatter.2.cloned.1.call-start = ((), (), s32[]{:S(2)}) async-start(), calls=%async_computation.3 | async-start | bytes 9437184 | tf_op jit(solution)/shard_map/reduce_scatter | solution.py:173
  30.5 0.6 copy-start
  37.5 11.7 %copy-start.1 = (s32[1,16]{1,0:T(1,128)S(1)}, s32[1,16]{1,0:T(1,128)}, u32[]{:S(2)}) copy-start(s32[1,16]{1,0:T(1,128)} %param.9) | copy-start | bytes 196
  37.5 115.0 %all-to-all-start.1 = ((bf16[32,64,1152]{2,1,0:T(8,128)(2,1)}), bf16[32,64,1152]{2,1,0:T(8,128)(2,1)}, u32[]{:S(2)}, u32[]{:S(2)}) async-start(bf16[32,64,1152]{2,1,0:T(8,128)(2,1)} %shard_map.55), calls=%async_computation.1 | async-start | bytes 9437184 | tf_op jit(solution)/shard_map/all_to_all | solution.py:172
  49.1 139.9 %all-gather.3.cloned.1.call-start = ((), (), s32[]{:S(2)}) async-start(), calls=%async_computation.4 | async-start | bytes 2359296 | tf_op jit(solution)/shard_map/all_gather | solution.py:176
Sparse Core Ops, SparseCore 0:
  37.6 58.4 reduce-scatter.1
  159.7 29.2 all-gather.2

commit v2 on v0

v2 whole, which is shorter than its diff:
```python
import jax
import jax.numpy as jnp
from jax import lax
from jax.experimental import pallas as pl
from jax.experimental.pallas import tpu as pltpu
from jax.sharding import PartitionSpec as P

BLOCK = 128


VMEM_LIMIT = pltpu.CompilerParams(vmem_limit_bytes=62 * 1024 * 1024)
SMEM_SPEC = pl.BlockSpec(memory_space=pltpu.SMEM)
HBM_SPEC = pl.BlockSpec(memory_space=pltpu.HBM)
VMEM_SPEC = pl.BlockSpec(memory_space=pltpu.VMEM)


def pick_kernel(ids_ref, src_ref, out_ref, buf, insem, outsem):
    slots = buf.shape[0]
    groups = insem.shape[0]
    size = slots // groups
    for s in range(slots):
        pltpu.make_async_copy(src_ref.at[ids_ref[s, 0]], buf.at[s], insem.at[s // size]).start()
    stores = []
    for g in range(groups):
        span = pl.ds(g * size, size)
        pltpu.make_async_copy(src_ref.at[span], buf.at[span], insem.at[g]).wait()
        stores.append(pltpu.make_async_copy(buf.at[span], out_ref.at[span], outsem.at[g]))
        stores[g].start()
    for store in stores:
        store.wait()


def pick(ids, src):
    groups = 4
    shape = (ids.shape[0],) + src.shape[1:]
    return pl.pallas_call(
        pick_kernel,
        out_shape=jax.ShapeDtypeStruct(shape, src.dtype),
        in_specs=[SMEM_SPEC, HBM_SPEC],
        out_specs=HBM_SPEC,
        scratch_shapes=[
            pltpu.VMEM(shape, src.dtype),
            pltpu.SemaphoreType.DMA((groups,)),
            pltpu.SemaphoreType.DMA((groups,)),
        ],
        compiler_params=VMEM_LIMIT,
    )(ids, src)


def down_kernel(owner_ref, tok_ref, recv_ref, part_ref, tok, fac, tsem, fsem):
    blocks = tok.shape[0]
    groups = tsem.shape[0]
    size = blocks // groups
    for g in range(groups):
        span = pl.ds(g * size, size)
        pltpu.make_async_copy(tok_ref.at[span], tok.at[span], tsem.at[g]).start()
        for b in range(g * size, (g + 1) * size):
            pltpu.make_async_copy(recv_ref.at[owner_ref[b]], fac.at[b], fsem.at[g]).start()
    for g in range(groups):
        span = pl.ds(g * size, size)
        pltpu.make_async_copy(recv_ref.at[span], fac.at[span], fsem.at[g]).wait()
        pltpu.make_async_copy(tok_ref.at[span], tok.at[span], tsem.at[g]).wait()
        for b in range(g * size, (g + 1) * size):
            part_ref[b] = lax.dot_general(
                fac[b],
                tok[b],
                (((1,), (1,)), ((), ())),
                preferred_element_type=jnp.float32,
            ).astype(jnp.bfloat16)


def down_products(owner, token_blocks, recv):
    groups = 4
    blocks, rows, feat = token_blocks.shape
    rank = recv.shape[1]
    return pl.pallas_call(
        down_kernel,
        out_shape=jax.ShapeDtypeStruct((blocks, rank, rows), jnp.bfloat16),
        in_specs=[SMEM_SPEC, HBM_SPEC, HBM_SPEC],
        out_specs=VMEM_SPEC,
        scratch_shapes=[
            pltpu.VMEM((blocks, rows, feat), jnp.bfloat16),
            pltpu.VMEM((blocks, rank, feat), jnp.bfloat16),
            pltpu.SemaphoreType.DMA((groups,)),
            pltpu.SemaphoreType.DMA((groups,)),
        ],
        compiler_params=VMEM_LIMIT,
    )(owner, token_blocks, recv)


def final_kernel(owner_ref, parts_ref, up_ref, base_ref, out_ref):
    shares, blocks, rank, rows = parts_ref.shape
    first = pl.program_id(0) * blocks
    for b in range(blocks):
        total = parts_ref[0, b].astype(jnp.float32)
        for s in range(1, shares):
            total += parts_ref[s, b].astype(jnp.float32)
        delta = lax.dot_general(
            total.astype(jnp.bfloat16),
            up_ref[owner_ref[first + b]],
            (((0,), (0,)), ((), ())),
            preferred_element_type=jnp.float32,
        )
        span = pl.ds(b * rows, rows)
        out_ref[span, :] = (base_ref[span, :] + delta).astype(jnp.bfloat16)


def finish(owner, parts, ups, base):
    shares, blocks, rank, rows = parts.shape
    wide = base.shape[1]
    step = blocks // 2
    return pl.pallas_call(
        final_kernel,
        out_shape=jax.ShapeDtypeStruct(base.shape, jnp.bfloat16),
        grid=(blocks // step,),
        in_specs=[
            SMEM_SPEC,
            pl.BlockSpec((shares, step, rank, rows), lambda i: (0, i, 0, 0)),
            pl.BlockSpec(ups.shape, lambda i: (0, 0, 0)),
            pl.BlockSpec((step * rows, wide), lambda i: (i, 0)),
        ],
        out_specs=pl.BlockSpec((step * rows, wide), lambda i: (i, 0)),
        compiler_params=VMEM_LIMIT,
    )(owner, parts, ups, base)


def local(
    tokens, value_projection_weight, adapter_down_factors, adapter_up_factors, block_adapter_table
):
    groups = lax.axis_size("dp")
    rows_dev, feat_dev = tokens.shape
    blocks = rows_dev // BLOCK
    adapter_per_device = adapter_down_factors.shape[0]
    ids = block_adapter_table[0]
    owner = ids // adapter_per_device
    hit = owner[None, :] == jnp.arange(groups, dtype=jnp.int32)[:, None]
    asked = jnp.sum(jnp.where(hit, (ids - owner * adapter_per_device)[None, :], 0), axis=1)
    wanted = lax.all_to_all(asked[:, None], "dp", split_axis=0, concat_axis=0, tiled=True)
    outgoing = pick(wanted, jnp.swapaxes(adapter_down_factors, 1, 2))
    base_part = jnp.dot(tokens, value_projection_weight, preferred_element_type=jnp.float32)
    outgoing, base_part = lax.optimization_barrier((outgoing, base_part))
    received = lax.all_to_all(outgoing, "dp", split_axis=0, concat_axis=0, tiled=True)
    base = lax.psum_scatter(base_part, "tensor", scatter_dimension=1, tiled=True)
    outgoing_up = pick(wanted, adapter_up_factors)
    received, base, outgoing_up = lax.optimization_barrier((received, base, outgoing_up))
    ups = lax.all_to_all(outgoing_up, "dp", split_axis=0, concat_axis=0, tiled=True)
    part = down_products(owner, tokens.reshape(blocks, BLOCK, feat_dev), received)
    parts = lax.all_gather(part, "tensor", axis=0)
    return finish(owner, parts, ups, base)


def solution(mesh):
    placed = (
        P("dp", "tensor"),
        P("tensor", None),
        P("dp", "tensor", None),
        P("dp", None, "tensor"),
        P("dp", None),
    )
    return jax.shard_map(
        local, mesh=mesh, in_specs=placed, out_specs=P("dp", "tensor"), check_vma=False
    )
```

time: 353 us -> 183 us (0.52)
  blocking collectives: 245 us -> 23.8 us
  waiting for transfers between devices: 15.7 us -> 93.7 us
  local copies, waits for them, and re-layouts: 19.4 us -> 1.3 us
  Pallas kernels: 0 us -> 17.1 us
  other arithmetic: 11.7 us -> 1.28 us
  matrix products: 18.8 us -> 10.6 us
  starting transfers between devices: 26 us -> 21.2 us
    all_gather x1 -> x0, blocking collectives: 208 us -> none  [local(): all_ids = lax.all_gather(block_adapter_table, 'dp', axis=0, tiled=True)]
    all_to_all x3 -> x2, waiting for transfers between devices: 15.6 us -> 88.4 us  [the longest x1 88.4 us: local(): lax.all_to_all(outgoing, 'dp', split_axis=0, concat_axis=0, tiled=True)]
    psum x1 -> x0, blocking collectives: 36.7 us -> none  [local(): lax.psum(down_projection_part, 'tensor').astype(jnp.bfloat16)]
    all_to_all x0 -> x1, blocking collectives: none -> 23.8 us  [local(): lax.all_to_all(outgoing_up, 'dp', split_axis=0, concat_axis=0, tiled=True)]
    pallas_call x0 -> x4, Pallas kernels: none -> 17.1 us  [the longest x2 8.77 us: pick(): pl.pallas_call(pick_kernel, out_shape=jax.ShapeDtypeStruct(shape, src.dty...]
    gather x5 -> x0, local copies, waits for them, and re-layouts: 16.8 us -> none  [the longest x1 7.13 us: local(): token_blocks[source] * present[:, None, None]]
    dot_general x2 -> x0, matrix products: 9.84 us -> none  [the longest x1 8.54 us: local(): jnp.einsum('kbd,kdr->kbr', received.reshape(groups * capacity, BLOCK, fea...]
    mul x2 -> x0, other arithmetic: 8.11 us -> none  [the longest x1 7.21 us: local(): token_blocks[source] * present[:, None, None]]
  transfers between devices with their start and end apart: 4 -> 4, of which waited for: 1 -> 2; matrix products, arithmetic and copies ran while one was open for 9% -> 6% of each run, Pallas kernels for 0% -> 2%
where the time goes in v2:
time: 183 us; the launch traced here: 182 us
  waiting for transfers between devices  93.7 us (51%)
  blocking collectives  23.8 us (13%)
  starting transfers between devices  21.2 us (12%)
  Pallas kernels  17.1 us (9%)
  between operations  13.5 us (7%)
  matrix products  10.6 us (6%)
    all_to_all x1, waiting for transfers between devices, local(): lax.all_to_all(outgoing, 'dp', split_axis=0, concat_axis=0, tiled=True)  88.4 us
    all_to_all x1, blocking collectives, local(): lax.all_to_all(outgoing_up, 'dp', split_axis=0, concat_axis=0, tiled=True)  23.8 us
    all_to_all x1, starting transfers between devices, local(): lax.all_to_all(asked[:, None], 'dp', split_axis=0, concat_axis=0, tiled=T...  11.9 us
    dot_general x1, matrix products, local(): jnp.dot(tokens, value_projection_weight, preferred_element_type=jnp.float32)  10.6 us
    all_to_all x1, starting transfers between devices, local(): lax.all_to_all(outgoing, 'dp', split_axis=0, concat_axis=0, tiled=True)  9.21 us
    pallas_call x2, Pallas kernels, pick(): pl.pallas_call(pick_kernel, out_shape=jax.ShapeDtypeStruct(shape, src.dty...  8.77 us
    pallas_call x1, Pallas kernels, down_products(): pl.pallas_call(down_kernel, out_shape=jax.ShapeDtypeStruct((blocks, rank,...  5.31 us
    all_gather x1, waiting for transfers between devices, local(): parts = lax.all_gather(part, 'tensor', axis=0)  5.21 us
  transfers between devices with their start and end apart: 4, of which 2 were waited for; matrix products, arithmetic and copies ran while one was open for 6% of the time, Pallas kernels for 2%

profile of v2, /device:TPU:1, one launch (start us, length us, event | category | flops | bytes accessed | tf_op | source)
XLA Modules:
  0.0 182.4 jit_solution(15362012063840199978)
XLA Ops:
  6.5 0.7 subtract_bitcast_fusion
  7.2 0.1 select_reduce_fusion
  7.3 0.7 copy.14
  8.0 11.9 %all-to-all-start = ((s32[32,1,1]{2,1,0:T(1,128)}), s32[32,1,1]{2,1,0:T(1,128)S(1)}, u32[]{:S(2)}, u32[]{:S(2)}) async-start(s32[32,1,1]{2,1,0:T(1,128)} %copy.14), calls=%async_computation | async-start | bytes 32768 | tf_op jit(solution)/shard_map/all_to_all | solution.py:138
  19.9 0.0 reduce-scatter.2.cloned.1.call-start
  19.9 10.6 %fusion = f32[2048,1024]{1,0:T(8,128)} fusion(bf16[2048,1024]{1,0:T(8,128)(2,1)} %param.5, bf16[1024,1024]{1,0:T(8,128)(2,1)} %param.6), kind=kOutput, calls=%fused_computation.12 | convolution fusion | flops 4294967296 | bytes 14680064 | tf_op jit(solution)/shard_map/dot_general | solution.py:140
  30.5 0.0 all-to-all-done
  30.5 0.0 copy-start.1
  30.5 0.6 copy-done.1
  31.1 5.8 %shard_map.55 = bf16[32,64,1024]{2,1,0:T(8,128)(2,1)} custom-call(s32[32,1]{1,0:T(8,128)} %bitcast.22, bf16[32,64,1024]{2,1,0:T(8,128)(2,1)} %bitcast.19), custom_call_target="tpu_custom_call" | custom-call | tf_op jit(solution)/shard_map/pallas_call | solution.py:36
  36.9 0.0 reduce-scatter.2.cloned.1.call-update
  37.0 0.0 copy-start.2
  37.0 9.2 %all-to-all-start.1 = ((bf16[32,64,1024]{2,1,0:T(8,128)(2,1)}), bf16[32,64,1024]{2,1,0:T(8,128)(2,1)}, u32[]{:S(2)}, u32[]{:S(2)}) async-start(bf16[32,64,1024]{2,1,0:T(8,128)(2,1)} %shard_map.55), calls=%async_computation.1 | async-start | bytes 8388608 | tf_op jit(solution)/shard_map/all_to_all | solution.py:142
  46.2 0.0 all-gather.3.cloned.1.call-start
  46.2 0.0 copy-done.2
  46.2 0.5 and_select_fusion.1.owner_ref
  46.8 3.0 %shard_map.56 = bf16[32,64,128]{2,1,0:T(8,128)(2,1)} custom-call(s32[32,1]{1,0:T(8,128)} %bitcast.23, bf16[32,64,128]{2,1,0:T(8,128)(2,1)} %src_ref.1), custom_call_target="tpu_custom_call" | custom-call | tf_op jit(solution)/shard_map/pallas_call | solution.py:36
  49.8 88.4 %all-to-all-done.1.recv_ref = bf16[32,64,1024]{2,1,0:T(8,128)(2,1)} async-done(((bf16[32,64,1024]{2,1,0:T(8,128)(2,1)}), bf16[32,64,1024]{2,1,0:T(8,128)(2,1)}, u32[]{:S(2)}, u32[]{:S(2)}) %all-to-all-start.1) | async-done | bytes 4194336 | tf_op jit(solution)/shard_map/all_to_all | solution.py:142
  138.2 0.0 reduce-scatter.2.cloned.1.call-done.base_ref
  138.2 0.0 copy-start
  138.2 5.3 %shard_map.57 = bf16[16,64,128]{2,1,0:T(8,128)(2,1)} custom-call(s32[16]{0:T(128)} %and_select_fusion.1.owner_ref, bf16[16,128,1024]{2,1,0:T(8,128)(2,1)} %bitcast.20, bf16[32,64,1024]{2,1,0:T(8,128)(2,1)} %all-to-all-done.1.recv_ref), custom_call_target="tpu_custom_call" | custom-call | tf_op jit(solution)/shard_map/pallas_call | solution.py:76
  143.5 0.0 all-gather.3.cloned.1.call-update
  143.5 0.0 copy-done
  143.6 23.8 %all_to_all.21.up_ref = bf16[32,64,128]{2,1,0:T(8,128)(2,1)} all-to-all(bf16[32,64,128]{2,1,0:T(8,128)(2,1)S(1)} %copy-done), channel_id=1, replica_groups=mesh['dp'=32,'tensor'=8] {'dp'}, dimensions={0} | all-to-all | bytes 1048576 | tf_op jit(solution)/shard_map/all_to_all | solution.py:146
  167.4 5.2 %all-gather.3.cloned.1.call-done = bf16[128,64,128]{2,1,0:T(8,128)(2,1)} async-done(((bf16[16,64,128]{2,1,0:T(8,128)(2,1)}), bf16[128,64,128]{2,1,0:T(8,128)(2,1)}) %all-gather.3.cloned.1.call-update) | async-done | bytes 2097168 | tf_op jit(solution)/shard_map/all_gather | solution.py:148
  172.6 3.0 %shard_map.58 = bf16[2048,128]{1,0:T(8,128)(2,1)} custom-call(s32[16]{0:T(128)} %and_select_fusion.1.owner_ref, bf16[8,16,64,128]{3,2,1,0:T(8,128)(2,1)} %bitcast.21, bf16[32,64,128]{2,1,0:T(8,128)(2,1)} %all_to_all.21.up_ref, f32[2048,128]{1,0:T(8,128)} %reduce-scatter.2.cloned.1.call-done.base_ref), custom_call_target="tpu_custom_call" | custom-call | tf_op jit(solution)/shard_map/pallas_call | solution.py:112
Async XLA Ops:
  8.0 22.6 %all-to-all-start = ((s32[32,1,1]{2,1,0:T(1,128)}), s32[32,1,1]{2,1,0:T(1,128)S(1)}, u32[]{:S(2)}, u32[]{:S(2)}) async-start(s32[32,1,1]{2,1,0:T(1,128)} %copy.14), calls=%async_computation | async-start | bytes 32768 | tf_op jit(solution)/shard_map/all_to_all | solution.py:138
  19.9 118.3 %reduce-scatter.2.cloned.1.call-start = ((), (), s32[]{:S(2)}) async-start(), calls=%async_computation.4 | async-start | bytes 9437184 | tf_op jit(solution)/shard_map/reduce_scatter | solution.py:143
  30.5 0.6 copy-start.1
  37.0 9.3 %copy-start.2 = (s32[1,16]{1,0:T(1,128)S(1)}, s32[1,16]{1,0:T(1,128)}, u32[]{:S(2)}) copy-start(s32[1,16]{1,0:T(1,128)} %param.9) | copy-start | bytes 196
  37.0 101.2 %all-to-all-start.1 = ((bf16[32,64,1024]{2,1,0:T(8,128)(2,1)}), bf16[32,64,1024]{2,1,0:T(8,128)(2,1)}, u32[]{:S(2)}, u32[]{:S(2)}) async-start(bf16[32,64,1024]{2,1,0:T(8,128)(2,1)} %shard_map.55), calls=%async_computation.1 | async-start | bytes 8388608 | tf_op jit(solution)/shard_map/all_to_all | solution.py:142
  46.2 126.4 %all-gather.3.cloned.1.call-start = ((), (), s32[]{:S(2)}) async-start(), calls=%async_computation.5 | async-start | bytes 2359296 | tf_op jit(solution)/shard_map/all_gather | solution.py:148
  138.2 5.3 %copy-start = (bf16[32,64,128]{2,1,0:T(8,128)(2,1)S(1)}, bf16[32,64,128]{2,1,0:T(8,128)(2,1)}, u32[]{:S(2)}) copy-start(bf16[32,64,128]{2,1,0:T(8,128)(2,1)} %shard_map.56) | copy-start | bytes 1572868
Sparse Core Ops, SparseCore 0:
  37.1 55.9 reduce-scatter.1
  143.7 28.8 all-gather.2

commit v3 on v2

v3 whole, which is shorter than its diff:
```python
import jax
import jax.numpy as jnp
from jax import lax
from jax.experimental import pallas as pl
from jax.experimental.pallas import tpu as pltpu
from jax.sharding import PartitionSpec as P

BLOCK = 128


VMEM_LIMIT = pltpu.CompilerParams(vmem_limit_bytes=62 * 1024 * 1024)
SMEM_SPEC = pl.BlockSpec(memory_space=pltpu.SMEM)
HBM_SPEC = pl.BlockSpec(memory_space=pltpu.HBM)
VMEM_SPEC = pl.BlockSpec(memory_space=pltpu.VMEM)


def pick_kernel(ids_ref, src_ref, out_ref, buf, insem, outsem):
    slots = buf.shape[0]
    groups = insem.shape[0]
    size = slots // groups
    for s in range(slots):
        pltpu.make_async_copy(src_ref.at[ids_ref[s, 0]], buf.at[s], insem.at[s // size]).start()
    stores = []
    for g in range(groups):
        span = pl.ds(g * size, size)
        pltpu.make_async_copy(src_ref.at[span], buf.at[span], insem.at[g]).wait()
        stores.append(pltpu.make_async_copy(buf.at[span], out_ref.at[span], outsem.at[g]))
        stores[g].start()
    for store in stores:
        store.wait()


def pick(ids, src):
    groups = 4
    shape = (ids.shape[0],) + src.shape[1:]
    return pl.pallas_call(
        pick_kernel,
        out_shape=jax.ShapeDtypeStruct(shape, src.dtype),
        in_specs=[SMEM_SPEC, HBM_SPEC],
        out_specs=HBM_SPEC,
        scratch_shapes=[
            pltpu.VMEM(shape, src.dtype),
            pltpu.SemaphoreType.DMA((groups,)),
            pltpu.SemaphoreType.DMA((groups,)),
        ],
        compiler_params=VMEM_LIMIT,
    )(ids, src)


def base_kernel(place_ref, tok_ref, wgt_ref, *rest):
    outs, cols = rest[:-1], rest[-1]
    steps = len(outs) // 2
    wide = outs[0].shape[1]
    y, core = place_ref[0], place_ref[1]

    @pl.when(pl.program_id(0) == 0)
    def _():
        for j in range(2 * steps):
            block = 2 * lax.rem(y + j % steps, steps) + (core if j < steps else 1 - core)
            start = pl.multiple_of(block * wide, wide)
            cols[:, j * wide : (j + 1) * wide] = wgt_ref[:, pl.ds(start, wide)]

    out = jnp.dot(tok_ref[...], cols[...], preferred_element_type=jnp.float32)
    for j in range(2 * steps):
        outs[j][...] = out[:, j * wide : (j + 1) * wide]


def base_products(place, tokens, weight, wide):
    rows, feat = tokens.shape
    values = weight.shape[1]
    tile = 256
    count = values // wide
    return pl.pallas_call(
        base_kernel,
        out_shape=tuple(jax.ShapeDtypeStruct((rows, wide), jnp.float32) for _ in range(count)),
        grid=(rows // tile,),
        in_specs=[
            SMEM_SPEC,
            pl.BlockSpec((tile, feat), lambda i: (i, 0)),
            pl.BlockSpec((feat, values), lambda i: (0, 0)),
        ],
        out_specs=tuple(pl.BlockSpec((tile, wide), lambda i: (i, 0)) for _ in range(count)),
        scratch_shapes=[pltpu.VMEM((feat, values), weight.dtype)],
        compiler_params=VMEM_LIMIT,
    )(place, tokens, weight)


def down_kernel(place_ref, owner_ref, tok_ref, recv_ref, keep_ref, give_ref, tok, fac, tsem, fsem):
    blocks = tok.shape[0]
    groups = tsem.shape[0]
    size = blocks // groups
    half = blocks // 2
    core = place_ref[1]
    firsts = []
    for g in range(groups):
        side = 1 - core if g * size < half else core
        firsts.append(side * half + g * size % half)
        first = pl.multiple_of(firsts[g], size)
        span = pl.ds(g * size, size)
        pltpu.make_async_copy(tok_ref.at[pl.ds(first, size)], tok.at[span], tsem.at[g]).start()
        for b in range(size):
            pltpu.make_async_copy(
                recv_ref.at[owner_ref[first + b]], fac.at[g * size + b], fsem.at[g]
            ).start()
    for g in range(groups):
        span = pl.ds(g * size, size)
        pltpu.make_async_copy(recv_ref.at[span], fac.at[span], fsem.at[g]).wait()
        pltpu.make_async_copy(tok_ref.at[span], tok.at[span], tsem.at[g]).wait()
        for b in range(g * size, (g + 1) * size):
            out = lax.dot_general(
                fac[b],
                tok[b],
                (((1,), (1,)), ((), ())),
                preferred_element_type=jnp.float32,
            )
            if b < half:
                give_ref[b] = out
            else:
                keep_ref[b - half] = out


def down_products(place, owner, token_blocks, recv):
    groups = 4
    blocks, rows, feat = token_blocks.shape
    rank = recv.shape[1]
    half = jax.ShapeDtypeStruct((blocks // 2, rank, rows), jnp.float32)
    return pl.pallas_call(
        down_kernel,
        out_shape=(half, half),
        in_specs=[SMEM_SPEC, SMEM_SPEC, HBM_SPEC, HBM_SPEC],
        out_specs=(VMEM_SPEC, VMEM_SPEC),
        scratch_shapes=[
            pltpu.VMEM((blocks, rows, feat), jnp.bfloat16),
            pltpu.VMEM((blocks, rank, feat), jnp.bfloat16),
            pltpu.SemaphoreType.DMA((groups,)),
            pltpu.SemaphoreType.DMA((groups,)),
        ],
        compiler_params=VMEM_LIMIT,
    )(place, owner, token_blocks, recv)


def final_kernel(place_ref, owner_ref, mine_ref, other_ref, up_ref, base_ref, out_ref):
    blocks, rank, rows = mine_ref.shape
    step = pl.program_id(0)
    own = step == place_ref[1]
    for b in range(blocks):
        low = jnp.where(own, mine_ref[b], other_ref[b])
        delta = lax.dot_general(
            low,
            up_ref[owner_ref[step * blocks + b]],
            (((0,), (0,)), ((), ())),
            preferred_element_type=jnp.float32,
        )
        span = pl.ds(b * rows, rows)
        out_ref[span, :] = (base_ref[span, :] + delta).astype(jnp.bfloat16)


def finish(place, owner, mine, other, ups, base):
    blocks, rank, rows = mine.shape
    wide = base.shape[1]
    half = pl.BlockSpec((blocks, rank, rows), lambda i: (0, 0, 0))
    return pl.pallas_call(
        final_kernel,
        out_shape=jax.ShapeDtypeStruct(base.shape, jnp.bfloat16),
        grid=(2,),
        in_specs=[
            SMEM_SPEC,
            SMEM_SPEC,
            half,
            half,
            pl.BlockSpec(ups.shape, lambda i: (0, 0, 0)),
            pl.BlockSpec((blocks * rows, wide), lambda i: (i, 0)),
        ],
        out_specs=pl.BlockSpec((blocks * rows, wide), lambda i: (i, 0)),
        compiler_params=VMEM_LIMIT,
    )(place, owner, mine, other, ups, base)


def local(
    tokens, value_projection_weight, adapter_down_factors, adapter_up_factors, block_adapter_table
):
    groups = lax.axis_size("dp")
    shares = lax.axis_size("tensor")
    chips = shares // 2
    me = lax.axis_index("tensor")
    place = jnp.stack([me // 2, me % 2]).astype(jnp.int32)
    swap = [(i, i ^ 1) for i in range(shares)]
    columns = [[2 * y + c for y in range(chips)] for c in range(2)]
    rows_dev, feat_dev = tokens.shape
    wide = adapter_up_factors.shape[2]
    blocks = rows_dev // BLOCK
    adapter_per_device = adapter_down_factors.shape[0]
    ids = block_adapter_table[0]
    owner = ids // adapter_per_device
    hit = owner[None, :] == jnp.arange(groups, dtype=jnp.int32)[:, None]
    asked = jnp.sum(jnp.where(hit, (ids - owner * adapter_per_device)[None, :], 0), axis=1)
    wanted = lax.all_to_all(asked[:, None], "dp", split_axis=0, concat_axis=0, tiled=True)
    outgoing = pick(wanted, jnp.swapaxes(adapter_down_factors, 1, 2))
    products = base_products(place, tokens, value_projection_weight, wide)
    outgoing, products = lax.optimization_barrier((outgoing, products))
    received = lax.all_to_all(outgoing, "dp", split_axis=0, concat_axis=0, tiled=True)

    sums = {}
    for k in (2, 1, 3, 0):
        sums[k] = products[k] + lax.ppermute(products[chips + k], "tensor", swap)
        if k:
            along = [(i, 2 * ((i // 2 + k) % chips) + i % 2) for i in range(shares)]
            sums[k] = lax.ppermute(sums[k], "tensor", along)
    base = (sums[0] + sums[1]) + (sums[2] + sums[3])

    outgoing_up = pick(wanted, adapter_up_factors)
    received, base, outgoing_up = lax.optimization_barrier((received, base, outgoing_up))
    ups = lax.all_to_all(outgoing_up, "dp", split_axis=0, concat_axis=0, tiled=True)
    keep, give = down_products(place, owner, tokens.reshape(blocks, BLOCK, feat_dev), received)
    part = (keep + lax.ppermute(give, "tensor", swap)).astype(jnp.bfloat16)
    parts = lax.all_gather(part, "tensor", axis=0, axis_index_groups=columns)
    mine = jnp.sum(parts.astype(jnp.float32), axis=0).astype(jnp.bfloat16)
    other = lax.ppermute(mine, "tensor", swap)
    return finish(place, owner, mine, other, ups, base)


def solution(mesh):
    placed = (
        P("dp", "tensor"),
        P("tensor", None),
        P("dp", "tensor", None),
        P("dp", None, "tensor"),
        P("dp", None),
    )
    return jax.shard_map(
        local, mesh=mesh, in_specs=placed, out_specs=P("dp", "tensor"), check_vma=False
    )
```

time: 183 us -> 170 us (0.929)
  starting transfers between devices: 21.2 us -> 40.8 us
  waiting for transfers between devices: 93.7 us -> 78.4 us
  between operations: 13.5 us -> 0.17 us
  blocking collectives: 23.8 us -> 11.2 us
  matrix products: 10.6 us -> 0 us
  Pallas kernels: 17.1 us -> 26.7 us
  other arithmetic: 1.28 us -> 8.97 us
    all_to_all x1, waiting for transfers between devices: 88.4 us -> 32.4 us  [local(): lax.all_to_all(outgoing, 'dp', split_axis=0, concat_axis=0, tiled=True)]
    ppermute x0 -> x9, waiting for transfers between devices: none -> 46 us  [the longest x3 40.3 us: local(): sums[k] = lax.ppermute(sums[k], 'tensor', along)]
    all_to_all x1 -> x0, blocking collectives: 23.8 us -> none  [local(): lax.all_to_all(outgoing_up, 'dp', split_axis=0, concat_axis=0, tiled=True)]
    all_gather x0 -> x1, blocking collectives: none -> 11.2 us  [local(): parts = lax.all_gather(part, 'tensor', axis=0, axis_index_groups=columns)]
    ppermute x0 -> x9, starting transfers between devices: none -> 10.9 us  [the longest x3 4.83 us: local(): sums[k] = lax.ppermute(sums[k], 'tensor', along)]
    dot_general x1 -> x0, matrix products: 10.6 us -> none  [local(): jnp.dot(tokens, value_projection_weight, preferred_element_type=jnp.float32)]
    pallas_call x1 -> x2, Pallas kernels: 5.31 us -> 15.8 us  [the longest x1 10.6 us: base_products(): pl.pallas_call(base_kernel, out_shape=tuple((jax.ShapeDtypeStruct((rows,...]
    all_to_all x0 -> x1, starting transfers between devices: none -> 8.51 us  [local(): lax.all_to_all(outgoing_up, 'dp', split_axis=0, concat_axis=0, tiled=True)]
  transfers between devices with their start and end apart: 4 -> 12, of which waited for: 2 -> 7; matrix products, arithmetic and copies ran while one was open for 6% -> 5% of each run, Pallas kernels for 2% -> 11%
where the time goes in v3:
time: 170 us; the launch traced here: 169 us
  waiting for transfers between devices  78.4 us (46%)
  starting transfers between devices  40.8 us (24%)
  Pallas kernels  26.7 us (16%)
  blocking collectives  11.2 us (7%)
  other arithmetic  8.97 us (5%)
  local copies, waits for them, and re-layouts  2.77 us (2%)
    ppermute x3, waiting for transfers between devices, local(): sums[k] = lax.ppermute(sums[k], 'tensor', along)  40.3 us
    all_to_all x1, waiting for transfers between devices, local(): lax.all_to_all(outgoing, 'dp', split_axis=0, concat_axis=0, tiled=True)  32.4 us
    all_to_all x1, starting transfers between devices, local(): lax.all_to_all(asked[:, None], 'dp', split_axis=0, concat_axis=0, tiled=T...  11.9 us
    all_gather x1, blocking collectives, local(): parts = lax.all_gather(part, 'tensor', axis=0, axis_index_groups=columns)  11.2 us
    pallas_call x1, Pallas kernels, base_products(): pl.pallas_call(base_kernel, out_shape=tuple((jax.ShapeDtypeStruct((rows,...  10.6 us
    all_to_all x1, starting transfers between devices, local(): lax.all_to_all(outgoing, 'dp', split_axis=0, concat_axis=0, tiled=True)  9.54 us
    all_to_all x1, starting transfers between devices, local(): lax.all_to_all(outgoing_up, 'dp', split_axis=0, concat_axis=0, tiled=True)  8.51 us
    pallas_call x2, Pallas kernels, pick(): pl.pallas_call(pick_kernel, out_shape=jax.ShapeDtypeStruct(shape, src.dty...  8.33 us
  transfers between devices with their start and end apart: 12, of which 7 were waited for; matrix products, arithmetic and copies ran while one was open for 5% of the time, Pallas kernels for 11%

profile of v3, /device:TPU:1, one launch (start us, length us, event | category | flops | bytes accessed | tf_op | source)
XLA Modules:
  0.0 169.1 jit_solution(11110344529160232826)
XLA Ops:
  0.0 0.7 subtract_bitcast_fusion
  0.7 0.1 select_reduce_fusion
  0.8 0.7 copy.14
  1.5 11.9 %all-to-all-start = ((s32[32,1,1]{2,1,0:T(1,128)}), s32[32,1,1]{2,1,0:T(1,128)S(1)}, u32[]{:S(2)}, u32[]{:S(2)}) async-start(s32[32,1,1]{2,1,0:T(1,128)} %copy.14), calls=%async_computation | async-start | bytes 32768 | tf_op jit(solution)/shard_map/all_to_all | solution.py:197
  13.3 0.6 pad_add_fusion.place_ref
  13.9 10.6 %shard_map.56 = (f32[2048,128]{1,0:T(8,128)}, f32[2048,128]{1,0:T(8,128)}, f32[2048,128]{1,0:T(8,128)}, f32[2048,128]{1,0:T(8,128)}, f32[2048,128]{1,0:T(8,128)}...) custom-call(s32[2]{0:T(128)} %pad_add_fusion.place_ref, bf16[2048,1024]{1,0:T(8,128)(2,1)} %tok_ref.1, ...), custom_call_target="tpu_custom_call" | custom-call | tf_op jit(solution)/shard_map/pallas_call | solution.py:73
  24.6 0.0 all-to-all-done
  24.6 0.6 copy-done.5
  25.2 5.5 %shard_map.55 = bf16[32,64,1024]{2,1,0:T(8,128)(2,1)} custom-call(s32[32,1]{1,0:T(8,128)} %bitcast.21, bf16[32,64,1024]{2,1,0:T(8,128)(2,1)} %bitcast.19), custom_call_target="tpu_custom_call" | custom-call | tf_op jit(solution)/shard_map/pallas_call | solution.py:36
  30.6 0.0 copy-start.7
  30.7 0.0 copy-start.3
  30.7 0.0 copy-start.2
  30.7 9.5 %all-to-all-start.1 = ((bf16[32,64,1024]{2,1,0:T(8,128)(2,1)}), bf16[32,64,1024]{2,1,0:T(8,128)(2,1)}, u32[]{:S(2)}, u32[]{:S(2)}) async-start(bf16[32,64,1024]{2,1,0:T(8,128)(2,1)} %shard_map.55), calls=%async_computation.1 | async-start | bytes 8388608 | tf_op jit(solution)/shard_map/all_to_all | solution.py:201
  40.2 1.6 collective-permute-start.1
  41.8 0.1 collective-permute-start.5
  41.9 0.4 collective-permute-start.3
  42.4 0.1 collective-permute-start
  42.5 2.2 %collective-permute-done.1 = f32[2048,128]{1,0:T(8,128)S(1)} collective-permute-done((f32[2048,128]{1,0:T(8,128)S(1)}, f32[2048,128]{1,0:T(8,128)S(1)}, u32[]{:S(2)}, u32[]{:S(2)}) %collective-permute-start.1) | collective-permute-done | bytes 1048608 | tf_op jit(solution)/shard_map/ppermute | solution.py:205
  44.6 0.1 add.34
  44.7 1.4 collective-permute-start.2
  46.1 1.1 collective-permute-done.5
  47.2 0.0 copy-done.2
  47.2 1.1 add.37
  48.3 2.7 %collective-permute-start.6 = (f32[2048,128]{1,0:T(8,128)}, f32[2048,128]{1,0:T(8,128)}, u32[]{:S(2)}, u32[]{:S(2)}) collective-permute-start(f32[2048,128]{1,0:T(8,128)} %add.37), channel_id=1, source_target_pairs={{0,6},{1,7},{2,0},{3,1},{4,2},{5,3},{6,4},{7,5},{8,14},{9,15},{10,... | collective-permute-start | bytes 3145736 | tf_op jit(solution)/shard_map/ppermute | solution.py:208
  51.0 0.0 collective-permute-done.3
  51.0 1.1 add.36
  52.1 0.7 collective-permute-start.4
  52.9 2.9 %shard_map.57 = bf16[32,64,128]{2,1,0:T(8,128)(2,1)} custom-call(s32[32,1]{1,0:T(8,128)} %bitcast.22, bf16[32,64,128]{2,1,0:T(8,128)(2,1)} %src_ref.1), custom_call_target="tpu_custom_call" | custom-call | tf_op jit(solution)/shard_map/pallas_call | solution.py:36
  55.7 0.0 collective-permute-done
  55.8 14.9 %collective-permute-done.2 = f32[2048,128]{1,0:T(8,128)} collective-permute-done((f32[2048,128]{1,0:T(8,128)S(1)}, f32[2048,128]{1,0:T(8,128)}, u32[]{:S(2)}, u32[]{:S(2)}) %collective-permute-start.2) | collective-permute-done | bytes 1048608 | tf_op jit(solution)/shard_map/ppermute | solution.py:208
  70.6 25.5 %collective-permute-done.6 = f32[2048,128]{1,0:T(8,128)} collective-permute-done((f32[2048,128]{1,0:T(8,128)}, f32[2048,128]{1,0:T(8,128)}, u32[]{:S(2)}, u32[]{:S(2)}) %collective-permute-start.6) | collective-permute-done | bytes 1048608 | tf_op jit(solution)/shard_map/ppermute | solution.py:208
  96.1 0.0 collective-permute-done.4
  96.1 3.7 %add_add_fusion.base_ref = f32[2048,128]{1,0:T(8,128)} fusion(f32[2048,128]{1,0:T(8,128)} %collective-permute-done.4, f32[2048,128]{1,0:T(8,128)} %collective-permute-done.6, f32[2048,128]{1,0:T(8,128)} %collective-permute-done.2, f32[2048,128]{1,0:T(8,128)} %get-tuple-element.36, f32[2048,128]{1,0:T(8,128)} %collective-permute-done), kind=kLoop, calls=%fused_computation | loop fusion | flops 1048576 | bytes 6291456 | tf_op jit(solution)/shard_map/add | solution.py:209
  99.8 32.4 %all-to-all-done.1.recv_ref = bf16[32,64,1024]{2,1,0:T(8,128)(2,1)} async-done(((bf16[32,64,1024]{2,1,0:T(8,128)(2,1)}), bf16[32,64,1024]{2,1,0:T(8,128)(2,1)}, u32[]{:S(2)}, u32[]{:S(2)}) %all-to-all-start.1) | async-done | bytes 4194336 | tf_op jit(solution)/shard_map/all_to_all | solution.py:201
  132.2 8.5 %all-to-all-start.2 = ((bf16[32,64,128]{2,1,0:T(8,128)(2,1)}), bf16[32,64,128]{2,1,0:T(8,128)(2,1)S(1)}, u32[]{:S(2)}, u32[]{:S(2)}) async-start(bf16[32,64,128]{2,1,0:T(8,128)(2,1)} %shard_map.57), calls=%async_computation.2 | async-start | bytes 1048576 | tf_op jit(solution)/shard_map/all_to_all | solution.py:213
  140.8 0.6 and_select_fusion.1.owner_ref
  141.3 5.2 %shard_map.58 = (f32[8,64,128]{2,1,0:T(8,128)}, f32[8,64,128]{2,1,0:T(8,128)}) custom-call(s32[2]{0:T(128)} %pad_add_fusion.place_ref, s32[16]{0:T(128)} %and_select_fusion.1.owner_ref, bf16[16,128,1024]{2,1,0:T(8,128)(2,1)} %bitcast.18, bf16[32,64,1024]{2,1,0:T(8,128)(2,1)} %all-to-all-done.1.recv_ref), custom_call_target="tpu_custom_call" | custom-call | tf_op jit(solution)/shard_map/pallas_call | solution.py:127
  146.5 1.3 collective-permute-start.7
  147.8 1.4 collective-permute-done.7
  149.2 1.0 add_convert_fusion
  150.2 11.2 %all-gather = bf16[32,64,128]{2,1,0:T(8,128)(2,1)S(1)} all-gather(bf16[8,64,128]{2,1,0:T(8,128)(2,1)S(1)} %add_convert_fusion), channel_id=2, replica_groups={{0,2,4,6},{1,3,5,7},{8,10,12,14},{9,11,13,15},{16,18,20,22},{17,19,21,2..., dimensions={0}, use_global_device_ids=true | all-gather | bytes 655360 | tf_op jit(solution)/shard_map/all_gather | solution.py:216
  161.4 0.1 reduce_sum.22.mine_ref
  161.5 2.5 %collective-permute-start.8 = (bf16[8,64,128]{2,1,0:T(8,128)(2,1)S(1)}, bf16[8,64,128]{2,1,0:T(8,128)(2,1)S(1)}, u32[]{:S(2)}, u32[]{:S(2)}) collective-permute-start(bf16[8,64,128]{2,1,0:T(8,128)(2,1)S(1)} %reduce_sum.22.mine_ref), channel_id=1, source_target_pairs={{0,1},{1,0},{2,3},{3,2},{4,5},{5,4},{6,7},{7,6},{8,9},{9,8},{10,11... | collective-permute-start | bytes 393224 | tf_op jit(solution)/shard_map/ppermute | solution.py:218
  164.1 1.0 collective-permute-done.8.other_ref
  165.1 0.0 all-to-all-done.2.up_ref
  165.1 0.6 copy-done.6
  165.7 0.8 copy-done
  166.5 2.6 %shard_map.59 = bf16[2048,128]{1,0:T(8,128)(2,1)} custom-call(s32[2]{0:T(128)} %pad_add_fusion.place_ref, s32[16]{0:T(128)} %and_select_fusion.1.owner_ref, bf16[8,64,128]{2,1,0:T(8,128)(2,1)} %copy-done.4, bf16[8,64,128]{2,1,0:T(8,128)(2,1)} %copy-done.6, bf16[32,64,128]{2,1,0:T(8,128)(2,1)} %copy-done, f32[2048,128]{1,0:T(8,128)} %add_add_fusion.base_ref), custom_call_target="tpu_custom_call" | custom-call | tf_op jit(solution)/shard_map/pallas_call | solution.py:162
  (11 shorter events, 0.0 us)
Async XLA Ops:
  1.5 23.1 %all-to-all-start = ((s32[32,1,1]{2,1,0:T(1,128)}), s32[32,1,1]{2,1,0:T(1,128)S(1)}, u32[]{:S(2)}, u32[]{:S(2)}) async-start(s32[32,1,1]{2,1,0:T(1,128)} %copy.14), calls=%async_computation | async-start | bytes 32768 | tf_op jit(solution)/shard_map/all_to_all | solution.py:197
  24.6 0.6 copy-start.5
  30.6 9.6 %copy-start.7 = (f32[2048,128]{1,0:T(8,128)S(1)}, f32[2048,128]{1,0:T(8,128)}, u32[]{:S(2)}) copy-start(f32[2048,128]{1,0:T(8,128)} %get-tuple-element.39) | copy-start | bytes 3145732
  30.7 14.0 %copy-start.3 = (f32[2048,128]{1,0:T(8,128)S(1)}, f32[2048,128]{1,0:T(8,128)}, u32[]{:S(2)}) copy-start(f32[2048,128]{1,0:T(8,128)} %get-tuple-element.38) | copy-start | bytes 3145732
  30.7 16.6 %copy-start.2 = (f32[2048,128]{1,0:T(8,128)S(1)}, f32[2048,128]{1,0:T(8,128)}, u32[]{:S(2)}) copy-start(f32[2048,128]{1,0:T(8,128)} %get-tuple-element.42) | copy-start | bytes 3145732
  30.7 101.6 %all-to-all-start.1 = ((bf16[32,64,1024]{2,1,0:T(8,128)(2,1)}), bf16[32,64,1024]{2,1,0:T(8,128)(2,1)}, u32[]{:S(2)}, u32[]{:S(2)}) async-start(bf16[32,64,1024]{2,1,0:T(8,128)(2,1)} %shard_map.55), calls=%async_computation.1 | async-start | bytes 8388608 | tf_op jit(solution)/shard_map/all_to_all | solution.py:201
  40.2 10.8 %copy-start.1 = (f32[2048,128]{1,0:T(8,128)S(1)}, f32[2048,128]{1,0:T(8,128)}, u32[]{:S(2)}) copy-start(f32[2048,128]{1,0:T(8,128)} %get-tuple-element.40) | copy-start | bytes 3145732
  40.2 4.4 %collective-permute-start.1 = (f32[2048,128]{1,0:T(8,128)S(1)}, f32[2048,128]{1,0:T(8,128)S(1)}, u32[]{:S(2)}, u32[]{:S(2)}) collective-permute-start(f32[2048,128]{1,0:T(8,128)S(1)} %copy-done.7), channel_id=1, source_target_pairs={{0,1},{1,0},{2,3},{3,2},{4,5},{5,4},{6,7},{7,6},{8,9},{9,8},{10,11... | collective-permute-start | bytes 3145736 | tf_op jit(solution)/shard_map/ppermute | solution.py:205
  41.8 5.4 %collective-permute-start.5 = (f32[2048,128]{1,0:T(8,128)}, f32[2048,128]{1,0:T(8,128)S(1)}, u32[]{:S(2)}, u32[]{:S(2)}) collective-permute-start(f32[2048,128]{1,0:T(8,128)} %get-tuple-element.43), channel_id=1, source_target_pairs={{0,1},{1,0},{2,3},{3,2},{4,5},{5,4},{6,7},{7,6},{8,9},{9,8},{10,11... | collective-permute-start | bytes 3145736 | tf_op jit(solution)/shard_map/ppermute | solution.py:205
  41.9 9.1 %collective-permute-start.3 = (f32[2048,128]{1,0:T(8,128)}, f32[2048,128]{1,0:T(8,128)S(1)}, u32[]{:S(2)}, u32[]{:S(2)}) collective-permute-start(f32[2048,128]{1,0:T(8,128)} %get-tuple-element.41), channel_id=1, source_target_pairs={{0,1},{1,0},{2,3},{3,2},{4,5},{5,4},{6,7},{7,6},{8,9},{9,8},{10,11... | collective-permute-start | bytes 3145736 | tf_op jit(solution)/shard_map/ppermute | solution.py:205
  42.4 13.4 %collective-permute-start = (f32[2048,128]{1,0:T(8,128)}, f32[2048,128]{1,0:T(8,128)}, u32[]{:S(2)}, u32[]{:S(2)}) collective-permute-start(f32[2048,128]{1,0:T(8,128)} %get-tuple-element.37), channel_id=1, source_target_pairs={{0,1},{1,0},{2,3},{3,2},{4,5},{5,4},{6,7},{7,6},{8,9},{9,8},{10,11... | collective-permute-start | bytes 3145736 | tf_op jit(solution)/shard_map/ppermute | solution.py:205
  44.7 25.9 %collective-permute-start.2 = (f32[2048,128]{1,0:T(8,128)S(1)}, f32[2048,128]{1,0:T(8,128)}, u32[]{:S(2)}, u32[]{:S(2)}) collective-permute-start(f32[2048,128]{1,0:T(8,128)S(1)} %add.34), channel_id=1, source_target_pairs={{0,2},{1,3},{2,4},{3,5},{4,6},{5,7},{6,0},{7,1},{8,10},{9,11},{10,... | collective-permute-start | bytes 3145736 | tf_op jit(solution)/shard_map/ppermute | solution.py:208
  48.3 47.8 %collective-permute-start.6 = (f32[2048,128]{1,0:T(8,128)}, f32[2048,128]{1,0:T(8,128)}, u32[]{:S(2)}, u32[]{:S(2)}) collective-permute-start(f32[2048,128]{1,0:T(8,128)} %add.37), channel_id=1, source_target_pairs={{0,6},{1,7},{2,0},{3,1},{4,2},{5,3},{6,4},{7,5},{8,14},{9,15},{10,... | collective-permute-start | bytes 3145736 | tf_op jit(solution)/shard_map/ppermute | solution.py:208
  52.1 88.6 %copy-start.8 = (s32[1,16]{1,0:T(1,128)S(1)}, s32[1,16]{1,0:T(1,128)}, u32[]{:S(2)}) copy-start(s32[1,16]{1,0:T(1,128)} %param.9) | copy-start | bytes 196
  52.1 44.0 %collective-permute-start.4 = (f32[2048,128]{1,0:T(8,128)}, f32[2048,128]{1,0:T(8,128)}, u32[]{:S(2)}, u32[]{:S(2)}) collective-permute-start(f32[2048,128]{1,0:T(8,128)} %add.36), channel_id=1, source_target_pairs={{0,4},{1,5},{2,6},{3,7},{4,0},{5,1},{6,2},{7,3},{8,12},{9,13},{10,... | collective-permute-start | bytes 3145736 | tf_op jit(solution)/shard_map/ppermute | solution.py:208
  132.2 32.8 %all-to-all-start.2 = ((bf16[32,64,128]{2,1,0:T(8,128)(2,1)}), bf16[32,64,128]{2,1,0:T(8,128)(2,1)S(1)}, u32[]{:S(2)}, u32[]{:S(2)}) async-start(bf16[32,64,128]{2,1,0:T(8,128)(2,1)} %shard_map.57), calls=%async_computation.2 | async-start | bytes 1048576 | tf_op jit(solution)/shard_map/all_to_all | solution.py:213
  146.5 2.7 %collective-permute-start.7 = (f32[8,64,128]{2,1,0:T(8,128)}, f32[8,64,128]{2,1,0:T(8,128)S(1)}, u32[]{:S(2)}, u32[]{:S(2)}) collective-permute-start(f32[8,64,128]{2,1,0:T(8,128)} %get-tuple-element.46), channel_id=1, source_target_pairs={{0,1},{1,0},{2,3},{3,2},{4,5},{5,4},{6,7},{7,6},{8,9},{9,8},{10,11... | collective-permute-start | bytes 786440 | tf_op jit(solution)/shard_map/ppermute | solution.py:215
  161.5 3.5 %copy-start.4 = (bf16[8,64,128]{2,1,0:T(8,128)(2,1)}, bf16[8,64,128]{2,1,0:T(8,128)(2,1)S(1)}, u32[]{:S(2)}) copy-start(bf16[8,64,128]{2,1,0:T(8,128)(2,1)S(1)} %reduce_sum.22.mine_ref) | copy-start | bytes 393220
  161.5 3.5 %collective-permute-start.8 = (bf16[8,64,128]{2,1,0:T(8,128)(2,1)S(1)}, bf16[8,64,128]{2,1,0:T(8,128)(2,1)S(1)}, u32[]{:S(2)}, u32[]{:S(2)}) collective-permute-start(bf16[8,64,128]{2,1,0:T(8,128)(2,1)S(1)} %reduce_sum.22.mine_ref), channel_id=1, source_target_pairs={{0,1},{1,0},{2,3},{3,2},{4,5},{5,4},{6,7},{7,6},{8,9},{9,8},{10,11... | collective-permute-start | bytes 393224 | tf_op jit(solution)/shard_map/ppermute | solution.py:218
  165.1 0.7 copy-start.6
  165.7 0.8 copy-start

commit v4 on v3

--- a/solution.py
+++ b/solution.py
@@ -8,42 +8,31 @@
 BLOCK = 128
 
 
-VMEM_LIMIT = pltpu.CompilerParams(vmem_limit_bytes=62 * 1024 * 1024)
+def grant(mib):
+    return pltpu.CompilerParams(vmem_limit_bytes=mib * 1024 * 1024)
+
+
 SMEM_SPEC = pl.BlockSpec(memory_space=pltpu.SMEM)
 HBM_SPEC = pl.BlockSpec(memory_space=pltpu.HBM)
 VMEM_SPEC = pl.BlockSpec(memory_space=pltpu.VMEM)
 
 
-def pick_kernel(ids_ref, src_ref, out_ref, buf, insem, outsem):
-    slots = buf.shape[0]
-    groups = insem.shape[0]
-    size = slots // groups
+def pick_kernel(ids_ref, src_ref, out_ref, sem):
+    slots = out_ref.shape[0]
     for s in range(slots):
-        pltpu.make_async_copy(src_ref.at[ids_ref[s, 0]], buf.at[s], insem.at[s // size]).start()
-    stores = []
-    for g in range(groups):
-        span = pl.ds(g * size, size)
-        pltpu.make_async_copy(src_ref.at[span], buf.at[span], insem.at[g]).wait()
-        stores.append(pltpu.make_async_copy(buf.at[span], out_ref.at[span], outsem.at[g]))
-        stores[g].start()
-    for store in stores:
-        store.wait()
+        pltpu.make_async_copy(src_ref.at[ids_ref[s, 0]], out_ref.at[s], sem).start()
+    pltpu.make_async_copy(src_ref, out_ref, sem).wait()
 
 
 def pick(ids, src):
-    groups = 4
-    shape = (ids.shape[0],) + src.shape[1:]
+    assert ids.shape[0] == src.shape[0]
     return pl.pallas_call(
         pick_kernel,
-        out_shape=jax.ShapeDtypeStruct(shape, src.dtype),
-        in_specs=[SMEM_SPEC, HBM_SPEC],
+        out_shape=jax.ShapeDtypeStruct(src.shape, src.dtype),
+        in_specs=[SMEM_SPEC, VMEM_SPEC],
         out_specs=HBM_SPEC,
-        scratch_shapes=[
-            pltpu.VMEM(shape, src.dtype),
-            pltpu.SemaphoreType.DMA((groups,)),
-            pltpu.SemaphoreType.DMA((groups,)),
-        ],
-        compiler_params=VMEM_LIMIT,
+        scratch_shapes=[pltpu.SemaphoreType.DMA(())],
+        compiler_params=grant(52),
     )(ids, src)
 
 
@@ -81,35 +70,26 @@
         ],
         out_specs=tuple(pl.BlockSpec((tile, wide), lambda i: (i, 0)) for _ in range(count)),
         scratch_shapes=[pltpu.VMEM((feat, values), weight.dtype)],
-        compiler_params=VMEM_LIMIT,
+        compiler_params=grant(20),
     )(place, tokens, weight)
 
 
-def down_kernel(place_ref, owner_ref, tok_ref, recv_ref, keep_ref, give_ref, tok, fac, tsem, fsem):
-    blocks = tok.shape[0]
-    groups = tsem.shape[0]
+def down_kernel(place_ref, owner_ref, tok_ref, recv_ref, keep_ref, give_ref, fac, sem):
+    blocks = fac.shape[0]
+    groups = sem.shape[0]
     size = blocks // groups
     half = blocks // 2
     core = place_ref[1]
-    firsts = []
-    for g in range(groups):
-        side = 1 - core if g * size < half else core
-        firsts.append(side * half + g * size % half)
-        first = pl.multiple_of(firsts[g], size)
-        span = pl.ds(g * size, size)
-        pltpu.make_async_copy(tok_ref.at[pl.ds(first, size)], tok.at[span], tsem.at[g]).start()
-        for b in range(size):
-            pltpu.make_async_copy(
-                recv_ref.at[owner_ref[first + b]], fac.at[g * size + b], fsem.at[g]
-            ).start()
+    order = [(1 - core if b < half else core) * half + b % half for b in range(blocks)]
+    for b in range(blocks):
+        pltpu.make_async_copy(recv_ref.at[owner_ref[order[b]]], fac.at[b], sem.at[b // size]).start()
     for g in range(groups):
         span = pl.ds(g * size, size)
-        pltpu.make_async_copy(recv_ref.at[span], fac.at[span], fsem.at[g]).wait()
-        pltpu.make_async_copy(tok_ref.at[span], tok.at[span], tsem.at[g]).wait()
+        pltpu.make_async_copy(recv_ref.at[span], fac.at[span], sem.at[g]).wait()
         for b in range(g * size, (g + 1) * size):
             out = lax.dot_general(
                 fac[b],
-                tok[b],
+                tok_ref[order[b]],
                 (((1,), (1,)), ((), ())),
                 preferred_element_type=jnp.float32,
             )
@@ -127,15 +107,13 @@
     return pl.pallas_call(
         down_kernel,
         out_shape=(half, half),
-        in_specs=[SMEM_SPEC, SMEM_SPEC, HBM_SPEC, HBM_SPEC],
+        in_specs=[SMEM_SPEC, SMEM_SPEC, VMEM_SPEC, HBM_SPEC],
         out_specs=(VMEM_SPEC, VMEM_SPEC),
         scratch_shapes=[
-            pltpu.VMEM((blocks, rows, feat), jnp.bfloat16),
             pltpu.VMEM((blocks, rank, feat), jnp.bfloat16),
             pltpu.SemaphoreType.DMA((groups,)),
-            pltpu.SemaphoreType.DMA((groups,)),
         ],
-        compiler_params=VMEM_LIMIT,
+        compiler_params=grant(52),
     )(place, owner, token_blocks, recv)
 
 
@@ -172,7 +150,7 @@
             pl.BlockSpec((blocks * rows, wide), lambda i: (i, 0)),
         ],
         out_specs=pl.BlockSpec((blocks * rows, wide), lambda i: (i, 0)),
-        compiler_params=VMEM_LIMIT,
+        compiler_params=grant(24),
     )(place, owner, mine, other, ups, base)
 
 
@@ -196,10 +174,10 @@
     asked = jnp.sum(jnp.where(hit, (ids - owner * adapter_per_device)[None, :], 0), axis=1)
     wanted = lax.all_to_all(asked[:, None], "dp", split_axis=0, concat_axis=0, tiled=True)
     outgoing = pick(wanted, jnp.swapaxes(adapter_down_factors, 1, 2))
+    received = lax.all_to_all(outgoing, "dp", split_axis=0, concat_axis=0, tiled=True)
+
+    tokens, outgoing_up = lax.optimization_barrier((tokens, pick(wanted, adapter_up_factors)))
     products = base_products(place, tokens, value_projection_weight, wide)
-    outgoing, products = lax.optimization_barrier((outgoing, products))
-    received = lax.all_to_all(outgoing, "dp", split_axis=0, concat_axis=0, tiled=True)
-
     sums = {}
     for k in (2, 1, 3, 0):
         sums[k] = products[k] + lax.ppermute(products[chips + k], "tensor", swap)
@@ -208,7 +186,6 @@
             sums[k] = lax.ppermute(sums[k], "tensor", along)
     base = (sums[0] + sums[1]) + (sums[2] + sums[3])
 
-    outgoing_up = pick(wanted, adapter_up_factors)
     received, base, outgoing_up = lax.optimization_barrier((received, base, outgoing_up))
     ups = lax.all_to_all(outgoing_up, "dp", split_axis=0, concat_axis=0, tiled=True)
     keep, give = down_products(place, owner, tokens.reshape(blocks, BLOCK, feat_dev), received)

time: 170 us -> 156 us (0.918)
  blocking collectives: 11.2 us -> 31.5 us
  starting transfers between devices: 40.8 us -> 25.7 us
  other arithmetic: 8.97 us -> 1.59 us
  Pallas kernels: 26.7 us -> 19.7 us
  waiting for transfers between devices: 78.4 us -> 74.9 us
    all_to_all x0 -> x1, blocking collectives: none -> 20.2 us  [local(): lax.all_to_all(asked[:, None], 'dp', split_axis=0, concat_axis=0, tiled=T...]
    all_to_all x1 -> x0, starting transfers between devices: 11.9 us -> none  [local(): lax.all_to_all(asked[:, None], 'dp', split_axis=0, concat_axis=0, tiled=T...]
    all_to_all x1, waiting for transfers between devices: 32.4 us -> 27.6 us  [local(): lax.all_to_all(outgoing, 'dp', split_axis=0, concat_axis=0, tiled=True)]
    all_to_all x1, starting transfers between devices: 9.54 us -> 5 us  [local(): lax.all_to_all(outgoing, 'dp', split_axis=0, concat_axis=0, tiled=True)]
    pallas_call x1, Pallas kernels: 10.6 us -> 6.91 us  [base_products(): pl.pallas_call(base_kernel, out_shape=tuple((jax.ShapeDtypeStruct((rows,...]
    add x1, other arithmetic: 3.71 us -> 0.23 us  [local(): base = sums[0] + sums[1] + (sums[2] + sums[3])]
    ppermute x3, waiting for transfers between devices: 40.3 us -> 43.5 us  [local(): sums[k] = lax.ppermute(sums[k], 'tensor', along)]
    pallas_call x2, Pallas kernels: 8.33 us -> 5.76 us  [pick(): pl.pallas_call(pick_kernel, out_shape=jax.ShapeDtypeStruct(src.shape, src...]
  transfers between devices with their start and end apart: 12 -> 11, of which waited for: 7 -> 7; matrix products, arithmetic and copies ran while one was open for 5% -> 1% of each run, Pallas kernels for 11% -> 9%
where the time goes in v4:
time: 156 us
  waiting for transfers between devices  74.9 us (48%)
  blocking collectives  31.5 us (20%)
  starting transfers between devices  25.7 us (16%)
  Pallas kernels  19.7 us (13%)
  local copies, waits for them, and re-layouts  2.29 us (1%)
  other arithmetic  1.59 us (1%)
    ppermute x3, waiting for transfers between devices, local(): sums[k] = lax.ppermute(sums[k], 'tensor', along)  43.5 us
    all_to_all x1, waiting for transfers between devices, local(): lax.all_to_all(outgoing, 'dp', split_axis=0, concat_axis=0, tiled=True)  27.6 us
    all_to_all x1, blocking collectives, local(): lax.all_to_all(asked[:, None], 'dp', split_axis=0, concat_axis=0, tiled=T...  20.2 us
    all_gather x1, blocking collectives, local(): parts = lax.all_gather(part, 'tensor', axis=0, axis_index_groups=columns)  11.2 us
    pallas_call x1, Pallas kernels, base_products(): pl.pallas_call(base_kernel, out_shape=tuple((jax.ShapeDtypeStruct((rows,...  6.91 us
    all_to_all x1, starting transfers between devices, local(): lax.all_to_all(outgoing_up, 'dp', split_axis=0, concat_axis=0, tiled=True)  6.67 us
    pallas_call x2, Pallas kernels, pick(): pl.pallas_call(pick_kernel, out_shape=jax.ShapeDtypeStruct(src.shape, src...  5.76 us
    ppermute x3, starting transfers between devices, local(): sums[k] = lax.ppermute(sums[k], 'tensor', along)  5.72 us
  transfers between devices with their start and end apart: 11, of which 7 were waited for; matrix products, arithmetic and copies ran while one was open for 1% of the time, Pallas kernels for 9%

profile of v4, /device:TPU:1, one launch (start us, length us, event | category | flops | bytes accessed | tf_op | source)
XLA Modules:
  0.0 155.9 jit_solution(9743947665738225346)
XLA Ops:
  0.0 0.7 subtract_bitcast_fusion
  0.7 0.1 select_reduce_fusion
  0.8 0.1 copy.14
  0.8 20.2 %all_to_all.21 = s32[32,1,1]{2,1,0:T(1,128)S(1)} all-to-all(s32[32,1,1]{2,1,0:T(1,128)S(1)} %copy.14), channel_id=1, replica_groups=mesh['dp'=32,'tensor'=8] {'dp'}, dimensions={0} | all-to-all | bytes 256 | tf_op jit(solution)/shard_map/all_to_all | solution.py:175
  21.1 4.2 %shard_map.56 = bf16[32,64,1024]{2,1,0:T(8,128)(2,1)} custom-call(s32[32,1]{1,0:T(8,128)S(1)} %bitcast.19, bf16[32,64,1024]{2,1,0:T(8,128)(2,1)} %bitcast.21), custom_call_target="tpu_custom_call" | custom-call | tf_op jit(solution)/shard_map/pallas_call | solution.py:29
  25.3 0.0 copy-start.2
  25.3 0.0 copy-start.1
  25.3 5.0 %all-to-all-start.1 = ((bf16[32,64,1024]{2,1,0:T(8,128)(2,1)}), bf16[32,64,1024]{2,1,0:T(8,128)(2,1)}, u32[]{:S(2)}, u32[]{:S(2)}) async-start(bf16[32,64,1024]{2,1,0:T(8,128)(2,1)} %shard_map.56), calls=%async_computation.1 | async-start | bytes 8388608 | tf_op jit(solution)/shard_map/all_to_all | solution.py:177
  30.3 0.1 pad_add_fusion.place_ref
  30.4 0.0 copy-done.2
  30.4 1.6 %shard_map.55 = bf16[32,64,128]{2,1,0:T(8,128)(2,1)} custom-call(s32[32,1]{1,0:T(8,128)S(1)} %bitcast.20, bf16[32,64,128]{2,1,0:T(8,128)(2,1)S(1)} %copy-done.2), custom_call_target="tpu_custom_call" | custom-call | tf_op jit(solution)/shard_map/pallas_call | solution.py:29
  32.0 0.0 copy-done.1
  32.0 0.0 copy-start
  32.0 2.2 %copy-done = bf16[2048,1024]{1,0:T(8,128)(2,1)S(1)} copy-done((bf16[2048,1024]{1,0:T(8,128)(2,1)S(1)}, bf16[2048,1024]{1,0:T(8,128)(2,1)}, u32[]{:S(2)}) %copy-start) | copy-done | bytes 4194328
  34.2 6.9 %shard_map.57 = (f32[2048,128]{1,0:T(8,128)S(1)}, f32[2048,128]{1,0:T(8,128)S(1)}, f32[2048,128]{1,0:T(8,128)S(1)}, f32[2048,128]{1,0:T(8,128)S(1)}, f32[2048,12...) custom-call(s32[2]{0:T(128)S(1)} %pad_add_fusion.place_ref, ...), custom_call_target="tpu_custom_call" | custom-call | tf_op jit(solution)/shard_map/pallas_call | solution.py:62
  41.1 2.2 %collective-permute-start.1 = (f32[2048,128]{1,0:T(8,128)S(1)}, f32[2048,128]{1,0:T(8,128)S(1)}, u32[]{:S(2)}, u32[]{:S(2)}) collective-permute-start(f32[2048,128]{1,0:T(8,128)S(1)} %get-tuple-element.24), channel_id=1, source_target_pairs={{0,1},{1,0},{2,3},{3,2},{4,5},{5,4},{6,7},{7,6},{8,9},{9,8},{10,11... | collective-permute-start | bytes 3145736 | tf_op jit(solution)/shard_map/ppermute | solution.py:183
  43.3 0.1 collective-permute-start.5
  43.4 0.4 collective-permute-start.3
  43.8 0.1 collective-permute-start
  43.9 1.7 %collective-permute-done.1 = f32[2048,128]{1,0:T(8,128)S(1)} collective-permute-done((f32[2048,128]{1,0:T(8,128)S(1)}, f32[2048,128]{1,0:T(8,128)S(1)}, u32[]{:S(2)}, u32[]{:S(2)}) %collective-permute-start.1) | collective-permute-done | bytes 1048608 | tf_op jit(solution)/shard_map/ppermute | solution.py:183
  45.6 0.1 add.34
  45.7 1.4 collective-permute-start.2
  47.1 0.0 collective-permute-done.5
  47.1 0.1 add.37
  47.2 2.8 %collective-permute-start.6 = (f32[2048,128]{1,0:T(8,128)S(1)}, f32[2048,128]{1,0:T(8,128)S(1)}, u32[]{:S(2)}, u32[]{:S(2)}) collective-permute-start(f32[2048,128]{1,0:T(8,128)S(1)} %add.37), channel_id=1, source_target_pairs={{0,6},{1,7},{2,0},{3,1},{4,2},{5,3},{6,4},{7,5},{8,14},{9,15},{10,... | collective-permute-start | bytes 3145736 | tf_op jit(solution)/shard_map/ppermute | solution.py:186
  50.0 0.0 collective-permute-done.3
  50.0 0.1 add.36
  50.2 0.0 copy-start.3
  50.2 1.5 collective-permute-start.4
  51.7 0.0 collective-permute-done
  51.7 19.9 %collective-permute-done.2 = f32[2048,128]{1,0:T(8,128)S(1)} collective-permute-done((f32[2048,128]{1,0:T(8,128)S(1)}, f32[2048,128]{1,0:T(8,128)S(1)}, u32[]{:S(2)}, u32[]{:S(2)}) %collective-permute-start.2) | collective-permute-done | bytes 1048608 | tf_op jit(solution)/shard_map/ppermute | solution.py:186
  71.6 22.9 %collective-permute-done.6 = f32[2048,128]{1,0:T(8,128)S(1)} collective-permute-done((f32[2048,128]{1,0:T(8,128)S(1)}, f32[2048,128]{1,0:T(8,128)S(1)}, u32[]{:S(2)}, u32[]{:S(2)}) %collective-permute-start.6) | collective-permute-done | bytes 1048608 | tf_op jit(solution)/shard_map/ppermute | solution.py:186
  94.5 0.7 collective-permute-done.4
  95.2 0.2 add_add_fusion.base_ref
  95.4 27.6 %all-to-all-done.1.recv_ref = bf16[32,64,1024]{2,1,0:T(8,128)(2,1)} async-done(((bf16[32,64,1024]{2,1,0:T(8,128)(2,1)}), bf16[32,64,1024]{2,1,0:T(8,128)(2,1)}, u32[]{:S(2)}, u32[]{:S(2)}) %all-to-all-start.1) | async-done | bytes 4194336 | tf_op jit(solution)/shard_map/all_to_all | solution.py:177
  123.0 6.7 %all-to-all-start.2 = ((bf16[32,64,128]{2,1,0:T(8,128)(2,1)}), bf16[32,64,128]{2,1,0:T(8,128)(2,1)S(1)}, u32[]{:S(2)}, u32[]{:S(2)}) async-start(bf16[32,64,128]{2,1,0:T(8,128)(2,1)} %shard_map.55), calls=%async_computation.2 | async-start | bytes 1048576 | tf_op jit(solution)/shard_map/all_to_all | solution.py:190
  129.7 0.0 copy-done.3
  129.7 5.3 %shard_map.58 = (f32[8,64,128]{2,1,0:T(8,128)S(1)}, f32[8,64,128]{2,1,0:T(8,128)S(1)}) custom-call(s32[2]{0:T(128)S(1)} %pad_add_fusion.place_ref, s32[16]{0:T(128)S(1)} %and_select_fusion.1.owner_ref, bf16[16,128,1024]{2,1,0:T(8,128)(2,1)} %bitcast.18, bf16[32,64,1024]{2,1,0:T(8,128)(2,1)} %all-to-all-done.1.recv_ref), custom_call_target="tpu_custom_call" | custom-call | tf_op jit(solution)/shard_map/pallas_call | solution.py:107
  135.0 3.0 %collective-permute-start.7 = (f32[8,64,128]{2,1,0:T(8,128)S(1)}, f32[8,64,128]{2,1,0:T(8,128)S(1)}, u32[]{:S(2)}, u32[]{:S(2)}) collective-permute-start(f32[8,64,128]{2,1,0:T(8,128)S(1)} %get-tuple-element.32), channel_id=1, source_target_pairs={{0,1},{1,0},{2,3},{3,2},{4,5},{5,4},{6,7},{7,6},{8,9},{9,8},{10,11... | collective-permute-start | bytes 786440 | tf_op jit(solution)/shard_map/ppermute | solution.py:192
  138.0 1.2 collective-permute-done.7
  139.2 11.2 %all-gather = bf16[32,64,128]{2,1,0:T(8,128)(2,1)S(1)} all-gather(bf16[8,64,128]{2,1,0:T(8,128)(2,1)S(1)} %add_convert_fusion), channel_id=2, replica_groups={{0,2,4,6},{1,3,5,7},{8,10,12,14},{9,11,13,15},{16,18,20,22},{17,19,21,2..., dimensions={0}, use_global_device_ids=true | all-gather | bytes 655360 | tf_op jit(solution)/shard_map/all_gather | solution.py:193
  150.4 0.1 reduce_sum.22.mine_ref
  150.5 2.5 %collective-permute-start.8 = (bf16[8,64,128]{2,1,0:T(8,128)(2,1)S(1)}, bf16[8,64,128]{2,1,0:T(8,128)(2,1)S(1)}, u32[]{:S(2)}, u32[]{:S(2)}) collective-permute-start(bf16[8,64,128]{2,1,0:T(8,128)(2,1)S(1)} %reduce_sum.22.mine_ref), channel_id=1, source_target_pairs={{0,1},{1,0},{2,3},{3,2},{4,5},{5,4},{6,7},{7,6},{8,9},{9,8},{10,11... | collective-permute-start | bytes 393224 | tf_op jit(solution)/shard_map/ppermute | solution.py:195
  153.1 1.0 collective-permute-done.8.other_ref
  154.0 0.0 all-to-all-done.2.up_ref
  154.0 1.8 %shard_map.59 = bf16[2048,128]{1,0:T(8,128)(2,1)} custom-call(s32[2]{0:T(128)S(1)} %pad_add_fusion.place_ref, s32[16]{0:T(128)S(1)} %and_select_fusion.1.owner_ref, bf16[8,64,128]{2,1,0:T(8,128)(2,1)S(1)} %reduce_sum.22.mine_ref, bf16[8,64,128]{2,1,0:T(8,128)(2,1)S(1)} %collective-permute-done.8.other_ref, bf16[32,64,128]{2,1,0:T(8,128)(2,1)S(1)} %all-to-all-done.2.up_ref, ...), custom_call_target="tpu_custom_call" | custom-call | tf_op jit(solution)/shard_map/pallas_call | solution.py:140
  (2 shorter events, 0.0 us)
Async XLA Ops:
  25.3 5.1 %copy-start.2 = (bf16[32,64,128]{2,1,0:T(8,128)(2,1)S(1)}, bf16[32,64,128]{2,1,0:T(8,128)(2,1)}, u32[]{:S(2)}) copy-start(bf16[32,64,128]{2,1,0:T(8,128)(2,1)} %src_ref.1) | copy-start | bytes 1572868
  25.3 6.7 %copy-start.1 = (bf16[1024,1024]{1,0:T(8,128)(2,1)S(1)}, bf16[1024,1024]{1,0:T(8,128)(2,1)}, u32[]{:S(2)}) copy-start(bf16[1024,1024]{1,0:T(8,128)(2,1)} %wgt_ref.1) | copy-start | bytes 6291460
  25.3 97.7 %all-to-all-start.1 = ((bf16[32,64,1024]{2,1,0:T(8,128)(2,1)}), bf16[32,64,1024]{2,1,0:T(8,128)(2,1)}, u32[]{:S(2)}, u32[]{:S(2)}) async-start(bf16[32,64,1024]{2,1,0:T(8,128)(2,1)} %shard_map.56), calls=%async_computation.1 | async-start | bytes 8388608 | tf_op jit(solution)/shard_map/all_to_all | solution.py:177
  32.0 2.2 %copy-start = (bf16[2048,1024]{1,0:T(8,128)(2,1)S(1)}, bf16[2048,1024]{1,0:T(8,128)(2,1)}, u32[]{:S(2)}) copy-start(bf16[2048,1024]{1,0:T(8,128)(2,1)} %tok_ref) | copy-start | bytes 12582916
  41.1 4.5 %collective-permute-start.1 = (f32[2048,128]{1,0:T(8,128)S(1)}, f32[2048,128]{1,0:T(8,128)S(1)}, u32[]{:S(2)}, u32[]{:S(2)}) collective-permute-start(f32[2048,128]{1,0:T(8,128)S(1)} %get-tuple-element.24), channel_id=1, source_target_pairs={{0,1},{1,0},{2,3},{3,2},{4,5},{5,4},{6,7},{7,6},{8,9},{9,8},{10,11... | collective-permute-start | bytes 3145736 | tf_op jit(solution)/shard_map/ppermute | solution.py:183
  43.3 3.8 %collective-permute-start.5 = (f32[2048,128]{1,0:T(8,128)S(1)}, f32[2048,128]{1,0:T(8,128)S(1)}, u32[]{:S(2)}, u32[]{:S(2)}) collective-permute-start(f32[2048,128]{1,0:T(8,128)S(1)} %get-tuple-element.28), channel_id=1, source_target_pairs={{0,1},{1,0},{2,3},{3,2},{4,5},{5,4},{6,7},{7,6},{8,9},{9,8},{10,11... | collective-permute-start | bytes 3145736 | tf_op jit(solution)/shard_map/ppermute | solution.py:183
  43.4 6.6 %collective-permute-start.3 = (f32[2048,128]{1,0:T(8,128)S(1)}, f32[2048,128]{1,0:T(8,128)S(1)}, u32[]{:S(2)}, u32[]{:S(2)}) collective-permute-start(f32[2048,128]{1,0:T(8,128)S(1)} %get-tuple-element.26), channel_id=1, source_target_pairs={{0,1},{1,0},{2,3},{3,2},{4,5},{5,4},{6,7},{7,6},{8,9},{9,8},{10,11... | collective-permute-start | bytes 3145736 | tf_op jit(solution)/shard_map/ppermute | solution.py:183
  43.8 7.9 %collective-permute-start = (f32[2048,128]{1,0:T(8,128)S(1)}, f32[2048,128]{1,0:T(8,128)S(1)}, u32[]{:S(2)}, u32[]{:S(2)}) collective-permute-start(f32[2048,128]{1,0:T(8,128)S(1)} %get-tuple-element.22), channel_id=1, source_target_pairs={{0,1},{1,0},{2,3},{3,2},{4,5},{5,4},{6,7},{7,6},{8,9},{9,8},{10,11... | collective-permute-start | bytes 3145736 | tf_op jit(solution)/shard_map/ppermute | solution.py:183
  45.7 25.9 %collective-permute-start.2 = (f32[2048,128]{1,0:T(8,128)S(1)}, f32[2048,128]{1,0:T(8,128)S(1)}, u32[]{:S(2)}, u32[]{:S(2)}) collective-permute-start(f32[2048,128]{1,0:T(8,128)S(1)} %add.34), channel_id=1, source_target_pairs={{0,2},{1,3},{2,4},{3,5},{4,6},{5,7},{6,0},{7,1},{8,10},{9,11},{10,... | collective-permute-start | bytes 3145736 | tf_op jit(solution)/shard_map/ppermute | solution.py:186
  47.2 47.3 %collective-permute-start.6 = (f32[2048,128]{1,0:T(8,128)S(1)}, f32[2048,128]{1,0:T(8,128)S(1)}, u32[]{:S(2)}, u32[]{:S(2)}) collective-permute-start(f32[2048,128]{1,0:T(8,128)S(1)} %add.37), channel_id=1, source_target_pairs={{0,6},{1,7},{2,0},{3,1},{4,2},{5,3},{6,4},{7,5},{8,14},{9,15},{10,... | collective-permute-start | bytes 3145736 | tf_op jit(solution)/shard_map/ppermute | solution.py:186
  50.2 79.5 %copy-start.3 = (s32[1,16]{1,0:T(1,128)S(1)}, s32[1,16]{1,0:T(1,128)}, u32[]{:S(2)}) copy-start(s32[1,16]{1,0:T(1,128)} %param.9) | copy-start | bytes 196
  50.2 45.0 %collective-permute-start.4 = (f32[2048,128]{1,0:T(8,128)S(1)}, f32[2048,128]{1,0:T(8,128)S(1)}, u32[]{:S(2)}, u32[]{:S(2)}) collective-permute-start(f32[2048,128]{1,0:T(8,128)S(1)} %add.36), channel_id=1, source_target_pairs={{0,4},{1,5},{2,6},{3,7},{4,0},{5,1},{6,2},{7,3},{8,12},{9,13},{10,... | collective-permute-start | bytes 3145736 | tf_op jit(solution)/shard_map/ppermute | solution.py:186
  123.0 31.0 %all-to-all-start.2 = ((bf16[32,64,128]{2,1,0:T(8,128)(2,1)}), bf16[32,64,128]{2,1,0:T(8,128)(2,1)S(1)}, u32[]{:S(2)}, u32[]{:S(2)}) async-start(bf16[32,64,128]{2,1,0:T(8,128)(2,1)} %shard_map.55), calls=%async_computation.2 | async-start | bytes 1048576 | tf_op jit(solution)/shard_map/all_to_all | solution.py:190
  135.0 4.2 %collective-permute-start.7 = (f32[8,64,128]{2,1,0:T(8,128)S(1)}, f32[8,64,128]{2,1,0:T(8,128)S(1)}, u32[]{:S(2)}, u32[]{:S(2)}) collective-permute-start(f32[8,64,128]{2,1,0:T(8,128)S(1)} %get-tuple-element.32), channel_id=1, source_target_pairs={{0,1},{1,0},{2,3},{3,2},{4,5},{5,4},{6,7},{7,6},{8,9},{9,8},{10,11... | collective-permute-start | bytes 786440 | tf_op jit(solution)/shard_map/ppermute | solution.py:192
  150.5 3.5 %collective-permute-start.8 = (bf16[8,64,128]{2,1,0:T(8,128)(2,1)S(1)}, bf16[8,64,128]{2,1,0:T(8,128)(2,1)S(1)}, u32[]{:S(2)}, u32[]{:S(2)}) collective-permute-start(bf16[8,64,128]{2,1,0:T(8,128)(2,1)S(1)} %reduce_sum.22.mine_ref), channel_id=1, source_target_pairs={{0,1},{1,0},{2,3},{3,2},{4,5},{5,4},{6,7},{7,6},{8,9},{9,8},{10,11... | collective-permute-start | bytes 393224 | tf_op jit(solution)/shard_map/ppermute | solution.py:195

commit v5 on v4

--- a/solution.py
+++ b/solution.py
@@ -173,10 +173,21 @@
     hit = owner[None, :] == jnp.arange(groups, dtype=jnp.int32)[:, None]
     asked = jnp.sum(jnp.where(hit, (ids - owner * adapter_per_device)[None, :], 0), axis=1)
     wanted = lax.all_to_all(asked[:, None], "dp", split_axis=0, concat_axis=0, tiled=True)
+    lines = 4
+    layers = groups // lines
+    my_line = lax.axis_index("dp") % lines
+    ring = jnp.arange(lines, dtype=jnp.int32)
     outgoing = pick(wanted, jnp.swapaxes(adapter_down_factors, 1, 2))
     received = lax.all_to_all(outgoing, "dp", split_axis=0, concat_axis=0, tiled=True)
 
-    tokens, outgoing_up = lax.optimization_barrier((tokens, pick(wanted, adapter_up_factors)))
+    by_line = wanted.reshape(layers, lines)[:, (my_line + ring) % lines].T.reshape(groups, 1)
+    up_lines = pick(by_line, adapter_up_factors).reshape((lines, layers) + adapter_up_factors.shape[1:])
+    tokens, up_lines = lax.optimization_barrier((tokens, up_lines))
+    moved = [up_lines[0]]
+    for d in range(1, lines):
+        along = [(i, i - i % lines + (i + d) % lines) for i in range(groups)]
+        moved.append(lax.ppermute(up_lines[d], "dp", along))
+    outgoing_up = jnp.stack(moved, axis=1)
     products = base_products(place, tokens, value_projection_weight, wide)
     sums = {}
     for k in (2, 1, 3, 0):
@@ -187,13 +198,17 @@
     base = (sums[0] + sums[1]) + (sums[2] + sums[3])
 
     received, base, outgoing_up = lax.optimization_barrier((received, base, outgoing_up))
-    ups = lax.all_to_all(outgoing_up, "dp", split_axis=0, concat_axis=0, tiled=True)
+    columns_z = [[z * lines + x for z in range(layers)] for x in range(lines)]
+    ups = lax.all_to_all(
+        outgoing_up, "dp", split_axis=0, concat_axis=0, tiled=True, axis_index_groups=columns_z
+    ).reshape((groups,) + adapter_up_factors.shape[1:])
+    up_slot = owner - owner % lines + (my_line - owner % lines) % lines
     keep, give = down_products(place, owner, tokens.reshape(blocks, BLOCK, feat_dev), received)
     part = (keep + lax.ppermute(give, "tensor", swap)).astype(jnp.bfloat16)
     parts = lax.all_gather(part, "tensor", axis=0, axis_index_groups=columns)
     mine = jnp.sum(parts.astype(jnp.float32), axis=0).astype(jnp.bfloat16)
     other = lax.ppermute(mine, "tensor", swap)
-    return finish(place, owner, mine, other, ups, base)
+    return finish(place, up_slot, mine, other, ups, base)
 
 
 def solution(mesh):

time: 156 us -> 155 us (level)
  waiting for transfers between devices: 74.9 us -> 66.8 us
  starting transfers between devices: 25.7 us -> 29.6 us
    ppermute x3, waiting for transfers between devices: 43.5 us -> 20.1 us  [local(): sums[k] = lax.ppermute(sums[k], 'tensor', along)]
    ppermute x0 -> x3, waiting for transfers between devices: none -> 16.8 us  [local(): moved.append(lax.ppermute(up_lines[d], 'dp', along))]
    ppermute x0 -> x3, starting transfers between devices: none -> 5.65 us  [local(): moved.append(lax.ppermute(up_lines[d], 'dp', along))]
    all_to_all x1, starting transfers between devices: 6.67 us -> 3.49 us  [local(): lax.all_to_all(outgoing_up, 'dp', split_axis=0, concat_axis=0, tiled=True...]
    all_to_all x1, waiting for transfers between devices: 27.6 us -> 26 us  [local(): lax.all_to_all(outgoing, 'dp', split_axis=0, concat_axis=0, tiled=True)]
  transfers between devices with their start and end apart: 11 -> 14, of which waited for: 7 -> 9; matrix products, arithmetic and copies ran while one was open for 1% -> 2% of each run, Pallas kernels for 9% -> 9%
where the time goes in v5:
time: 155 us; the launch traced here: 154 us
  waiting for transfers between devices  66.8 us (43%)
  blocking collectives  31.5 us (20%)
  starting transfers between devices  29.6 us (19%)
  Pallas kernels  19.8 us (13%)
  other arithmetic  3.14 us (2%)
  local copies, waits for them, and re-layouts  3.14 us (2%)
    all_to_all x1, waiting for transfers between devices, local(): lax.all_to_all(outgoing, 'dp', split_axis=0, concat_axis=0, tiled=True)  26 us
    all_to_all x1, blocking collectives, local(): lax.all_to_all(asked[:, None], 'dp', split_axis=0, concat_axis=0, tiled=T...  20.2 us
    ppermute x3, waiting for transfers between devices, local(): sums[k] = lax.ppermute(sums[k], 'tensor', along)  20.1 us
    ppermute x3, waiting for transfers between devices, local(): moved.append(lax.ppermute(up_lines[d], 'dp', along))  16.8 us
    all_gather x1, blocking collectives, local(): parts = lax.all_gather(part, 'tensor', axis=0, axis_index_groups=columns)  11.3 us
    pallas_call x1, Pallas kernels, base_products(): pl.pallas_call(base_kernel, out_shape=tuple((jax.ShapeDtypeStruct((rows,...  6.9 us
    pallas_call x2, Pallas kernels, pick(): pl.pallas_call(pick_kernel, out_shape=jax.ShapeDtypeStruct(src.shape, src...  5.8 us
    ppermute x3, starting transfers between devices, local(): sums[k] = lax.ppermute(sums[k], 'tensor', along)  5.76 us
  transfers between devices with their start and end apart: 14, of which 9 were waited for; matrix products, arithmetic and copies ran while one was open for 2% of the time, Pallas kernels for 9%

profile of v5, /device:TPU:1, one launch (start us, length us, event | category | flops | bytes accessed | tf_op | source)
XLA Modules:
  0.0 154.1 jit_solution(9385146407242174932)
XLA Ops:
  0.0 0.7 subtract_bitcast_fusion
  0.7 0.1 select_reduce_fusion
  0.8 0.1 copy.32
  0.8 20.2 %all_to_all.21 = s32[32,1,1]{2,1,0:T(1,128)S(1)} all-to-all(s32[32,1,1]{2,1,0:T(1,128)S(1)} %copy.32), channel_id=1, replica_groups=mesh['dp'=32,'tensor'=8] {'dp'}, dimensions={0} | all-to-all | bytes 256 | tf_op jit(solution)/shard_map/all_to_all | solution.py:175
  21.1 4.2 %shard_map.56 = bf16[32,64,1024]{2,1,0:T(8,128)(2,1)} custom-call(s32[32,1]{1,0:T(8,128)S(1)} %bitcast.43, bf16[32,64,1024]{2,1,0:T(8,128)(2,1)} %bitcast.44), custom_call_target="tpu_custom_call" | custom-call | tf_op jit(solution)/shard_map/pallas_call | solution.py:29
  25.3 0.0 copy-start.2
  25.3 5.0 %all-to-all-start.1 = ((bf16[32,64,1024]{2,1,0:T(8,128)(2,1)}), bf16[32,64,1024]{2,1,0:T(8,128)(2,1)}, u32[]{:S(2)}, u32[]{:S(2)}) async-start(bf16[32,64,1024]{2,1,0:T(8,128)(2,1)} %shard_map.56), calls=%async_computation.1 | async-start | bytes 8388608 | tf_op jit(solution)/shard_map/all_to_all | solution.py:181
  30.4 0.1 pad_add_fusion.place_ref
  30.5 0.7 reduce.1
  31.1 0.1 reshape.68
  31.2 0.1 copy.33
  31.3 0.6 gather_fusion
  31.8 0.1 reshape.82.ids_ref
  31.9 1.6 %shard_map.55 = bf16[32,64,128]{2,1,0:T(8,128)(2,1)S(1)} custom-call(s32[32,1]{1,0:T(8,128)S(1)} %reshape.82.ids_ref, bf16[32,64,128]{2,1,0:T(8,128)(2,1)S(1)} %copy-done.2), custom_call_target="tpu_custom_call" | custom-call | tf_op jit(solution)/shard_map/pallas_call | solution.py:29
  33.6 2.2 %copy-done = bf16[2048,1024]{1,0:T(8,128)(2,1)S(1)} copy-done((bf16[2048,1024]{1,0:T(8,128)(2,1)S(1)}, bf16[2048,1024]{1,0:T(8,128)(2,1)}, u32[]{:S(2)}) %copy-start) | copy-done | bytes 4194328
  35.7 6.9 %shard_map.57 = (f32[2048,128]{1,0:T(8,128)S(1)}, f32[2048,128]{1,0:T(8,128)S(1)}, f32[2048,128]{1,0:T(8,128)S(1)}, f32[2048,128]{1,0:T(8,128)S(1)}, f32[2048,12...) custom-call(s32[2]{0:T(128)S(1)} %pad_add_fusion.place_ref, ...), custom_call_target="tpu_custom_call" | custom-call | tf_op jit(solution)/shard_map/pallas_call | solution.py:62
  42.7 2.2 %collective-permute-start.1 = (f32[2048,128]{1,0:T(8,128)S(1)}, f32[2048,128]{1,0:T(8,128)S(1)}, u32[]{:S(2)}, u32[]{:S(2)}) collective-permute-start(f32[2048,128]{1,0:T(8,128)S(1)} %get-tuple-element.24), channel_id=1, source_target_pairs={{0,1},{1,0},{2,3},{3,2},{4,5},{5,4},{6,7},{7,6},{8,9},{9,8},{10,11... | collective-permute-start | bytes 3145736 | tf_op jit(solution)/shard_map/ppermute | solution.py:194
  44.9 0.1 collective-permute-start.5
  45.0 0.4 collective-permute-start.3
  45.4 0.1 collective-permute-start
  45.5 1.7 %collective-permute-done.1 = f32[2048,128]{1,0:T(8,128)S(1)} collective-permute-done((f32[2048,128]{1,0:T(8,128)S(1)}, f32[2048,128]{1,0:T(8,128)S(1)}, u32[]{:S(2)}, u32[]{:S(2)}) %collective-permute-start.1) | collective-permute-done | bytes 1048608 | tf_op jit(solution)/shard_map/ppermute | solution.py:194
  47.1 0.1 add.96
  47.2 1.4 collective-permute-start.2
  48.6 0.0 collective-permute-done.5
  48.6 0.1 add.99
  48.7 2.8 %collective-permute-start.6 = (f32[2048,128]{1,0:T(8,128)S(1)}, f32[2048,128]{1,0:T(8,128)S(1)}, u32[]{:S(2)}, u32[]{:S(2)}) collective-permute-start(f32[2048,128]{1,0:T(8,128)S(1)} %add.99), channel_id=1, source_target_pairs={{0,6},{1,7},{2,0},{3,1},{4,2},{5,3},{6,4},{7,5},{8,14},{9,15},{10,... | collective-permute-start | bytes 3145736 | tf_op jit(solution)/shard_map/ppermute | solution.py:197
  51.6 0.1 add.98
  51.7 1.6 %collective-permute-start.4 = (f32[2048,128]{1,0:T(8,128)S(1)}, f32[2048,128]{1,0:T(8,128)S(1)}, u32[]{:S(2)}, u32[]{:S(2)}) collective-permute-start(f32[2048,128]{1,0:T(8,128)S(1)} %add.98), channel_id=1, source_target_pairs={{0,4},{1,5},{2,6},{3,7},{4,0},{5,1},{6,2},{7,3},{8,12},{9,13},{10,... | collective-permute-start | bytes 3145736 | tf_op jit(solution)/shard_map/ppermute | solution.py:197
  53.3 1.4 collective-permute-start.7
  54.7 7.6 %collective-permute-done.7 = bf16[8,64,128]{2,1,0:T(8,128)(2,1)S(1)} collective-permute-done((bf16[8,64,128]{2,1,0:T(8,128)(2,1)S(1)}, bf16[8,64,128]{2,1,0:T(8,128)(2,1)S(1)}, u32[]{:S(2)}, u32[]{:S(2)}) %collective-permute-start.7) | collective-permute-done | bytes 131104 | tf_op jit(solution)/shard_map/ppermute | solution.py:189
  62.2 3.9 %collective-permute-start.8 = (bf16[8,64,128]{2,1,0:T(8,128)(2,1)S(1)}, bf16[8,64,128]{2,1,0:T(8,128)(2,1)S(1)}, u32[]{:S(2)}, u32[]{:S(2)}) collective-permute-start(bf16[8,64,128]{2,1,0:T(8,128)(2,1)S(1)} %get-tuple-element.41), channel_id=1, source_target_pairs={{0,16},{8,24},{16,0},{24,8},{32,48},{40,56},{48,32},{56,40},{64,80... | collective-permute-start | bytes 393224 | tf_op jit(solution)/shard_map/ppermute | solution.py:189
  66.1 5.1 %collective-permute-done.8 = bf16[8,64,128]{2,1,0:T(8,128)(2,1)S(1)} collective-permute-done((bf16[8,64,128]{2,1,0:T(8,128)(2,1)S(1)}, bf16[8,64,128]{2,1,0:T(8,128)(2,1)S(1)}, u32[]{:S(2)}, u32[]{:S(2)}) %collective-permute-start.8) | collective-permute-done | bytes 131104 | tf_op jit(solution)/shard_map/ppermute | solution.py:189
  71.2 0.4 collective-permute-start.9
  71.6 4.2 %collective-permute-done.9 = bf16[8,64,128]{2,1,0:T(8,128)(2,1)S(1)} collective-permute-done((bf16[8,64,128]{2,1,0:T(8,128)(2,1)S(1)}, bf16[8,64,128]{2,1,0:T(8,128)(2,1)S(1)}, u32[]{:S(2)}, u32[]{:S(2)}) %collective-permute-start.9) | collective-permute-done | bytes 131104 | tf_op jit(solution)/shard_map/ppermute | solution.py:189
  75.7 0.9 pad_maximum_fusion
  76.6 19.5 %collective-permute-done.6 = f32[2048,128]{1,0:T(8,128)S(1)} collective-permute-done((f32[2048,128]{1,0:T(8,128)S(1)}, f32[2048,128]{1,0:T(8,128)S(1)}, u32[]{:S(2)}, u32[]{:S(2)}) %collective-permute-start.6) | collective-permute-done | bytes 1048608 | tf_op jit(solution)/shard_map/ppermute | solution.py:197
  96.1 0.7 collective-permute-done.4
  96.7 0.3 add_add_fusion.base_ref
  97.0 26.0 %all-to-all-done.1.recv_ref = bf16[32,64,1024]{2,1,0:T(8,128)(2,1)} async-done(((bf16[32,64,1024]{2,1,0:T(8,128)(2,1)}), bf16[32,64,1024]{2,1,0:T(8,128)(2,1)}, u32[]{:S(2)}, u32[]{:S(2)}) %all-to-all-start.1) | async-done | bytes 4194336 | tf_op jit(solution)/shard_map/all_to_all | solution.py:181
  123.1 3.5 %all-to-all-start.2 = ((bf16[8,4,64,128]{3,2,1,0:T(8,128)(2,1)}), bf16[8,4,64,128]{3,2,1,0:T(8,128)(2,1)S(1)}, u32[]{:S(2)}, u32[]{:S(2)}) async-start(bf16[8,4,64,128]{3,2,1,0:T(8,128)(2,1)} %pad_maximum_fusion), calls=%async_computation.2 | async-start | bytes 1048576 | tf_op jit(solution)/shard_map/all_to_all | solution.py:202
  126.6 5.3 %shard_map.58 = (f32[8,64,128]{2,1,0:T(8,128)S(1)}, f32[8,64,128]{2,1,0:T(8,128)S(1)}) custom-call(s32[2]{0:T(128)S(1)} %pad_add_fusion.place_ref, s32[16]{0:T(128)S(1)} %get-tuple-element.38.owner_ref, bf16[16,128,1024]{2,1,0:T(8,128)(2,1)} %bitcast.40, bf16[32,64,1024]{2,1,0:T(8,128)(2,1)} %all-to-all-done.1.recv_ref), custom_call_target="tpu_custom_call" | custom-call | tf_op jit(solution)/shard_map/pallas_call | solution.py:107
  131.9 4.4 %collective-permute-start.10 = (f32[8,64,128]{2,1,0:T(8,128)S(1)}, f32[8,64,128]{2,1,0:T(8,128)S(1)}, u32[]{:S(2)}, u32[]{:S(2)}) collective-permute-start(f32[8,64,128]{2,1,0:T(8,128)S(1)} %get-tuple-element.32), channel_id=1, source_target_pairs={{0,1},{1,0},{2,3},{3,2},{4,5},{5,4},{6,7},{7,6},{8,9},{9,8},{10,11... | collective-permute-start | bytes 786440 | tf_op jit(solution)/shard_map/ppermute | solution.py:207
  136.3 1.2 collective-permute-done.10
  137.5 11.3 %all-gather = bf16[32,64,128]{2,1,0:T(8,128)(2,1)S(1)} all-gather(bf16[8,64,128]{2,1,0:T(8,128)(2,1)S(1)} %add_convert_fusion), channel_id=2, replica_groups={{0,2,4,6},{1,3,5,7},{8,10,12,14},{9,11,13,15},{16,18,20,22},{17,19,21,2..., dimensions={0}, use_global_device_ids=true | all-gather | bytes 655360 | tf_op jit(solution)/shard_map/all_gather | solution.py:208
  148.8 0.1 reduce_sum.22.mine_ref
  148.9 2.4 %collective-permute-start.11 = (bf16[8,64,128]{2,1,0:T(8,128)(2,1)S(1)}, bf16[8,64,128]{2,1,0:T(8,128)(2,1)S(1)}, u32[]{:S(2)}, u32[]{:S(2)}) collective-permute-start(bf16[8,64,128]{2,1,0:T(8,128)(2,1)S(1)} %reduce_sum.22.mine_ref), channel_id=1, source_target_pairs={{0,1},{1,0},{2,3},{3,2},{4,5},{5,4},{6,7},{7,6},{8,9},{9,8},{10,11... | collective-permute-start | bytes 393224 | tf_op jit(solution)/shard_map/ppermute | solution.py:210
  151.3 1.0 collective-permute-done.11.other_ref
  152.3 1.8 %shard_map.59 = bf16[2048,128]{1,0:T(8,128)(2,1)} custom-call(s32[2]{0:T(128)S(1)} %pad_add_fusion.place_ref, s32[16]{0:T(128)S(1)} %get-tuple-element.37.owner_ref, bf16[8,64,128]{2,1,0:T(8,128)(2,1)S(1)} %reduce_sum.22.mine_ref, bf16[8,64,128]{2,1,0:T(8,128)(2,1)S(1)} %collective-permute-done.11.other_ref, bf16[32,64,128]{2,1,0:T(8,128)(2,1)S(1)} %bitcast.42, ...), custom_call_target="tpu_custom_call" | custom-call | tf_op jit(solution)/shard_map/pallas_call | solution.py:140
  (15 shorter events, 0.1 us)
Async XLA Ops:
  25.3 6.6 %copy-start.2 = (bf16[32,64,128]{2,1,0:T(8,128)(2,1)S(1)}, bf16[32,64,128]{2,1,0:T(8,128)(2,1)}, u32[]{:S(2)}) copy-start(bf16[32,64,128]{2,1,0:T(8,128)(2,1)} %src_ref.1) | copy-start | bytes 1572868
  25.3 8.3 %copy-start.1 = (bf16[1024,1024]{1,0:T(8,128)(2,1)S(1)}, bf16[1024,1024]{1,0:T(8,128)(2,1)}, u32[]{:S(2)}) copy-start(bf16[1024,1024]{1,0:T(8,128)(2,1)} %wgt_ref.1) | copy-start | bytes 6291460
  25.3 97.7 %all-to-all-start.1 = ((bf16[32,64,1024]{2,1,0:T(8,128)(2,1)}), bf16[32,64,1024]{2,1,0:T(8,128)(2,1)}, u32[]{:S(2)}, u32[]{:S(2)}) async-start(bf16[32,64,1024]{2,1,0:T(8,128)(2,1)} %shard_map.56), calls=%async_computation.1 | async-start | bytes 8388608 | tf_op jit(solution)/shard_map/all_to_all | solution.py:181
  33.6 2.2 %copy-start = (bf16[2048,1024]{1,0:T(8,128)(2,1)S(1)}, bf16[2048,1024]{1,0:T(8,128)(2,1)}, u32[]{:S(2)}) copy-start(bf16[2048,1024]{1,0:T(8,128)(2,1)} %tok_ref) | copy-start | bytes 12582916
  42.7 4.5 %collective-permute-start.1 = (f32[2048,128]{1,0:T(8,128)S(1)}, f32[2048,128]{1,0:T(8,128)S(1)}, u32[]{:S(2)}, u32[]{:S(2)}) collective-permute-start(f32[2048,128]{1,0:T(8,128)S(1)} %get-tuple-element.24), channel_id=1, source_target_pairs={{0,1},{1,0},{2,3},{3,2},{4,5},{5,4},{6,7},{7,6},{8,9},{9,8},{10,11... | collective-permute-start | bytes 3145736 | tf_op jit(solution)/shard_map/ppermute | solution.py:194
  44.9 3.8 %collective-permute-start.5 = (f32[2048,128]{1,0:T(8,128)S(1)}, f32[2048,128]{1,0:T(8,128)S(1)}, u32[]{:S(2)}, u32[]{:S(2)}) collective-permute-start(f32[2048,128]{1,0:T(8,128)S(1)} %get-tuple-element.28), channel_id=1, source_target_pairs={{0,1},{1,0},{2,3},{3,2},{4,5},{5,4},{6,7},{7,6},{8,9},{9,8},{10,11... | collective-permute-start | bytes 3145736 | tf_op jit(solution)/shard_map/ppermute | solution.py:194
  45.0 6.6 %collective-permute-start.3 = (f32[2048,128]{1,0:T(8,128)S(1)}, f32[2048,128]{1,0:T(8,128)S(1)}, u32[]{:S(2)}, u32[]{:S(2)}) collective-permute-start(f32[2048,128]{1,0:T(8,128)S(1)} %get-tuple-element.26), channel_id=1, source_target_pairs={{0,1},{1,0},{2,3},{3,2},{4,5},{5,4},{6,7},{7,6},{8,9},{9,8},{10,11... | collective-permute-start | bytes 3145736 | tf_op jit(solution)/shard_map/ppermute | solution.py:194
  45.4 31.2 %collective-permute-start = (f32[2048,128]{1,0:T(8,128)S(1)}, f32[2048,128]{1,0:T(8,128)S(1)}, u32[]{:S(2)}, u32[]{:S(2)}) collective-permute-start(f32[2048,128]{1,0:T(8,128)S(1)} %get-tuple-element.22), channel_id=1, source_target_pairs={{0,1},{1,0},{2,3},{3,2},{4,5},{5,4},{6,7},{7,6},{8,9},{9,8},{10,11... | collective-permute-start | bytes 3145736 | tf_op jit(solution)/shard_map/ppermute | solution.py:194
  47.2 29.4 %collective-permute-start.2 = (f32[2048,128]{1,0:T(8,128)S(1)}, f32[2048,128]{1,0:T(8,128)S(1)}, u32[]{:S(2)}, u32[]{:S(2)}) collective-permute-start(f32[2048,128]{1,0:T(8,128)S(1)} %add.96), channel_id=1, source_target_pairs={{0,2},{1,3},{2,4},{3,5},{4,6},{5,7},{6,0},{7,1},{8,10},{9,11},{10,... | collective-permute-start | bytes 3145736 | tf_op jit(solution)/shard_map/ppermute | solution.py:197
  48.7 47.3 %collective-permute-start.6 = (f32[2048,128]{1,0:T(8,128)S(1)}, f32[2048,128]{1,0:T(8,128)S(1)}, u32[]{:S(2)}, u32[]{:S(2)}) collective-permute-start(f32[2048,128]{1,0:T(8,128)S(1)} %add.99), channel_id=1, source_target_pairs={{0,6},{1,7},{2,0},{3,1},{4,2},{5,3},{6,4},{7,5},{8,14},{9,15},{10,... | collective-permute-start | bytes 3145736 | tf_op jit(solution)/shard_map/ppermute | solution.py:197
  51.7 45.1 %collective-permute-start.4 = (f32[2048,128]{1,0:T(8,128)S(1)}, f32[2048,128]{1,0:T(8,128)S(1)}, u32[]{:S(2)}, u32[]{:S(2)}) collective-permute-start(f32[2048,128]{1,0:T(8,128)S(1)} %add.98), channel_id=1, source_target_pairs={{0,4},{1,5},{2,6},{3,7},{4,0},{5,1},{6,2},{7,3},{8,12},{9,13},{10,... | collective-permute-start | bytes 3145736 | tf_op jit(solution)/shard_map/ppermute | solution.py:197
  53.3 9.0 %collective-permute-start.7 = (bf16[8,64,128]{2,1,0:T(8,128)(2,1)S(1)}, bf16[8,64,128]{2,1,0:T(8,128)(2,1)S(1)}, u32[]{:S(2)}, u32[]{:S(2)}) collective-permute-start(bf16[8,64,128]{2,1,0:T(8,128)(2,1)S(1)} %get-tuple-element.42), channel_id=1, source_target_pairs={{0,8},{8,16},{16,24},{24,0},{32,40},{40,48},{48,56},{56,32},{64,72... | collective-permute-start | bytes 393224 | tf_op jit(solution)/shard_map/ppermute | solution.py:189
  62.2 9.0 %collective-permute-start.8 = (bf16[8,64,128]{2,1,0:T(8,128)(2,1)S(1)}, bf16[8,64,128]{2,1,0:T(8,128)(2,1)S(1)}, u32[]{:S(2)}, u32[]{:S(2)}) collective-permute-start(bf16[8,64,128]{2,1,0:T(8,128)(2,1)S(1)} %get-tuple-element.41), channel_id=1, source_target_pairs={{0,16},{8,24},{16,0},{24,8},{32,48},{40,56},{48,32},{56,40},{64,80... | collective-permute-start | bytes 393224 | tf_op jit(solution)/shard_map/ppermute | solution.py:189
  71.2 4.5 %collective-permute-start.9 = (bf16[8,64,128]{2,1,0:T(8,128)(2,1)S(1)}, bf16[8,64,128]{2,1,0:T(8,128)(2,1)S(1)}, u32[]{:S(2)}, u32[]{:S(2)}) collective-permute-start(bf16[8,64,128]{2,1,0:T(8,128)(2,1)S(1)} %get-tuple-element.40), channel_id=1, source_target_pairs={{0,24},{8,0},{16,8},{24,16},{32,56},{40,32},{48,40},{56,48},{64,88... | collective-permute-start | bytes 393224 | tf_op jit(solution)/shard_map/ppermute | solution.py:189
  75.7 50.8 %copy-start.3 = (s32[1,16]{1,0:T(1,128)S(1)}, s32[1,16]{1,0:T(1,128)}, u32[]{:S(2)}) copy-start(s32[1,16]{1,0:T(1,128)} %param.9) | copy-start | bytes 196
  123.1 29.2 %all-to-all-start.2 = ((bf16[8,4,64,128]{3,2,1,0:T(8,128)(2,1)}), bf16[8,4,64,128]{3,2,1,0:T(8,128)(2,1)S(1)}, u32[]{:S(2)}, u32[]{:S(2)}) async-start(bf16[8,4,64,128]{3,2,1,0:T(8,128)(2,1)} %pad_maximum_fusion), calls=%async_computation.2 | async-start | bytes 1048576 | tf_op jit(solution)/shard_map/all_to_all | solution.py:202
  131.9 5.6 %collective-permute-start.10 = (f32[8,64,128]{2,1,0:T(8,128)S(1)}, f32[8,64,128]{2,1,0:T(8,128)S(1)}, u32[]{:S(2)}, u32[]{:S(2)}) collective-permute-start(f32[8,64,128]{2,1,0:T(8,128)S(1)} %get-tuple-element.32), channel_id=1, source_target_pairs={{0,1},{1,0},{2,3},{3,2},{4,5},{5,4},{6,7},{7,6},{8,9},{9,8},{10,11... | collective-permute-start | bytes 786440 | tf_op jit(solution)/shard_map/ppermute | solution.py:207
  148.9 3.4 %collective-permute-start.11 = (bf16[8,64,128]{2,1,0:T(8,128)(2,1)S(1)}, bf16[8,64,128]{2,1,0:T(8,128)(2,1)S(1)}, u32[]{:S(2)}, u32[]{:S(2)}) collective-permute-start(bf16[8,64,128]{2,1,0:T(8,128)(2,1)S(1)} %reduce_sum.22.mine_ref), channel_id=1, source_target_pairs={{0,1},{1,0},{2,3},{3,2},{4,5},{5,4},{6,7},{7,6},{8,9},{9,8},{10,11... | collective-permute-start | bytes 393224 | tf_op jit(solution)/shard_map/ppermute | solution.py:210

commit v6 on v5

--- a/solution.py
+++ b/solution.py
@@ -17,10 +17,33 @@
 VMEM_SPEC = pl.BlockSpec(memory_space=pltpu.VMEM)
 
 
+def ask_kernel(table_ref, out_ref):
+    groups, _, lanes = out_ref.shape
+    share = out_ref.shape[0]
+    table = table_ref[...]
+    blocks = table.shape[1]
+    owner = lax.broadcasted_iota(jnp.int32, (groups, blocks), 0)
+    inside = jnp.broadcast_to(table, (groups, blocks)) - owner * share
+    hit = (inside >= 0) & (inside < share)
+    asked = jnp.sum(jnp.where(hit, inside, 0), axis=1, keepdims=True)
+    out_ref[...] = jnp.broadcast_to(asked, (groups, lanes)).reshape(groups, 1, lanes)
+
+
+def ask(table, groups, share):
+    assert groups == share
+    return pl.pallas_call(
+        ask_kernel,
+        out_shape=jax.ShapeDtypeStruct((groups, 1, 128), jnp.int32),
+        in_specs=[VMEM_SPEC],
+        out_specs=VMEM_SPEC,
+        compiler_params=grant(2),
+    )(table)
+
+
 def pick_kernel(ids_ref, src_ref, out_ref, sem):
     slots = out_ref.shape[0]
     for s in range(slots):
-        pltpu.make_async_copy(src_ref.at[ids_ref[s, 0]], out_ref.at[s], sem).start()
+        pltpu.make_async_copy(src_ref.at[ids_ref[s, 0, 0]], out_ref.at[s], sem).start()
     pltpu.make_async_copy(src_ref, out_ref, sem).wait()
 
 
@@ -86,17 +109,22 @@
     for g in range(groups):
         span = pl.ds(g * size, size)
         pltpu.make_async_copy(recv_ref.at[span], fac.at[span], sem.at[g]).wait()
-        for b in range(g * size, (g + 1) * size):
-            out = lax.dot_general(
-                fac[b],
-                tok_ref[order[b]],
-                (((1,), (1,)), ((), ())),
-                preferred_element_type=jnp.float32,
-            )
+        first = pl.multiple_of(order[g * size], size)
+        rank, feat = fac.shape[1:]
+        rows = tok_ref.shape[1]
+        out = lax.dot_general(
+            fac[span].reshape(size * rank, feat),
+            tok_ref[pl.ds(first, size)].reshape(size * rows, feat),
+            (((1,), (1,)), ((), ())),
+            preferred_element_type=jnp.float32,
+        )
+        for j in range(size):
+            b = g * size + j
+            pair = out[j * rank : (j + 1) * rank, j * rows : (j + 1) * rows]
             if b < half:
-                give_ref[b] = out
+                give_ref[b] = pair
             else:
-                keep_ref[b - half] = out
+                keep_ref[b - half] = pair
 
 
 def down_products(place, owner, token_blocks, recv):
@@ -170,9 +198,8 @@
     adapter_per_device = adapter_down_factors.shape[0]
     ids = block_adapter_table[0]
     owner = ids // adapter_per_device
-    hit = owner[None, :] == jnp.arange(groups, dtype=jnp.int32)[:, None]
-    asked = jnp.sum(jnp.where(hit, (ids - owner * adapter_per_device)[None, :], 0), axis=1)
-    wanted = lax.all_to_all(asked[:, None], "dp", split_axis=0, concat_axis=0, tiled=True)
+    asked = ask(block_adapter_table, groups, adapter_per_device)
+    wanted = lax.all_to_all(asked, "dp", split_axis=0, concat_axis=0, tiled=True)
     lines = 4
     layers = groups // lines
     my_line = lax.axis_index("dp") % lines
@@ -180,7 +207,8 @@
     outgoing = pick(wanted, jnp.swapaxes(adapter_down_factors, 1, 2))
     received = lax.all_to_all(outgoing, "dp", split_axis=0, concat_axis=0, tiled=True)
 
-    by_line = wanted.reshape(layers, lines)[:, (my_line + ring) % lines].T.reshape(groups, 1)
+    by_line = wanted.reshape(layers, lines, -1)[:, (my_line + ring) % lines]
+    by_line = jnp.swapaxes(by_line, 0, 1).reshape(wanted.shape)
     up_lines = pick(by_line, adapter_up_factors).reshape((lines, layers) + adapter_up_factors.shape[1:])
     tokens, up_lines = lax.optimization_barrier((tokens, up_lines))
     moved = [up_lines[0]]

time: 155 us -> 155 us (level)
  waiting for transfers between devices: 66.8 us -> 71.8 us
  starting transfers between devices: 29.6 us -> 25.6 us
    ppermute x3, waiting for transfers between devices: 16.8 us -> 23.5 us  [local(): moved.append(lax.ppermute(up_lines[d], 'dp', along))]
    ppermute x3, starting transfers between devices: 5.65 us -> 1.45 us  [local(): moved.append(lax.ppermute(up_lines[d], 'dp', along))]
    ppermute x3, waiting for transfers between devices: 20.1 us -> 17.6 us  [local(): sums[k] = lax.ppermute(sums[k], 'tensor', along)]
where the time goes in v6:
time: 155 us; the launch traced here: 154 us
  waiting for transfers between devices  71.8 us (46%)
  blocking collectives  31.5 us (20%)
  starting transfers between devices  25.6 us (17%)
  Pallas kernels  19.9 us (13%)
  local copies, waits for them, and re-layouts  3.44 us (2%)
  other arithmetic  1.82 us (1%)
    all_to_all x1, waiting for transfers between devices, local(): lax.all_to_all(outgoing, 'dp', split_axis=0, concat_axis=0, tiled=True)  26.8 us
    ppermute x3, waiting for transfers between devices, local(): moved.append(lax.ppermute(up_lines[d], 'dp', along))  23.5 us
    all_to_all x1, blocking collectives, local(): lax.all_to_all(asked, 'dp', split_axis=0, concat_axis=0, tiled=True)  20.2 us
    ppermute x3, waiting for transfers between devices, local(): sums[k] = lax.ppermute(sums[k], 'tensor', along)  17.6 us
    all_gather x1, blocking collectives, local(): parts = lax.all_gather(part, 'tensor', axis=0, axis_index_groups=columns)  11.2 us
    pallas_call x1, Pallas kernels, base_products(): pl.pallas_call(base_kernel, out_shape=tuple((jax.ShapeDtypeStruct((rows,...  6.91 us
    pallas_call x2, Pallas kernels, pick(): pl.pallas_call(pick_kernel, out_shape=jax.ShapeDtypeStruct(src.shape, src...  5.82 us
    ppermute x3, starting transfers between devices, local(): sums[k] = lax.ppermute(sums[k], 'tensor', along)  5.76 us
  transfers between devices with their start and end apart: 14, of which 9 were waited for; matrix products, arithmetic and copies ran while one was open for 2% of the time, Pallas kernels for 9%

profile of v6, /device:TPU:1, one launch (start us, length us, event | category | flops | bytes accessed | tf_op | source)
XLA Modules:
  0.0 154.1 jit_solution(17109463843006774269)
XLA Ops:
  0.0 0.7 copy-done.3
  0.7 0.1 shard_map.55
  0.8 20.2 %all_to_all.15.ids_ref = s32[32,1,128]{2,1,0:T(1,128)S(1)} all-to-all(s32[32,1,128]{2,1,0:T(1,128)S(1)} %shard_map.55), channel_id=1, replica_groups=mesh['dp'=32,'tensor'=8] {'dp'}, dimensions={0} | all-to-all | bytes 32768 | tf_op jit(solution)/shard_map/all_to_all | solution.py:202
  21.0 4.2 %shard_map.57 = bf16[32,64,1024]{2,1,0:T(8,128)(2,1)} custom-call(s32[32,1,128]{2,1,0:T(1,128)S(1)} %all_to_all.15.ids_ref, bf16[32,64,1024]{2,1,0:T(8,128)(2,1)} %bitcast.42), custom_call_target="tpu_custom_call" | custom-call | tf_op jit(solution)/shard_map/pallas_call | solution.py:52
  25.2 0.0 copy-start.2
  25.2 0.0 copy-start.1
  25.3 5.0 %all-to-all-start.1 = ((bf16[32,64,1024]{2,1,0:T(8,128)(2,1)}), bf16[32,64,1024]{2,1,0:T(8,128)(2,1)}, u32[]{:S(2)}, u32[]{:S(2)}) async-start(bf16[32,64,1024]{2,1,0:T(8,128)(2,1)} %shard_map.57), calls=%async_computation.1 | async-start | bytes 8388608 | tf_op jit(solution)/shard_map/all_to_all | solution.py:208
  30.3 0.1 pad_add_fusion.place_ref
  30.4 0.6 gather_fusion
  31.0 1.6 %shard_map.56 = bf16[32,64,128]{2,1,0:T(8,128)(2,1)S(1)} custom-call(s32[32,1,128]{2,1,0:T(1,128)S(1)} %bitcast.41, bf16[32,64,128]{2,1,0:T(8,128)(2,1)S(1)} %copy-done.2), custom_call_target="tpu_custom_call" | custom-call | tf_op jit(solution)/shard_map/pallas_call | solution.py:52
  32.6 0.0 copy-start
  32.6 2.2 %copy-done = bf16[2048,1024]{1,0:T(8,128)(2,1)S(1)} copy-done((bf16[2048,1024]{1,0:T(8,128)(2,1)S(1)}, bf16[2048,1024]{1,0:T(8,128)(2,1)}, u32[]{:S(2)}) %copy-start) | copy-done | bytes 4194328
  34.8 6.9 %shard_map.58 = (f32[2048,128]{1,0:T(8,128)S(1)}, f32[2048,128]{1,0:T(8,128)S(1)}, f32[2048,128]{1,0:T(8,128)S(1)}, f32[2048,128]{1,0:T(8,128)S(1)}, f32[2048,12...) custom-call(s32[2]{0:T(128)S(1)} %pad_add_fusion.place_ref, ...), custom_call_target="tpu_custom_call" | custom-call | tf_op jit(solution)/shard_map/pallas_call | solution.py:85
  41.7 2.2 %collective-permute-start.1 = (f32[2048,128]{1,0:T(8,128)S(1)}, f32[2048,128]{1,0:T(8,128)S(1)}, u32[]{:S(2)}, u32[]{:S(2)}) collective-permute-start(f32[2048,128]{1,0:T(8,128)S(1)} %get-tuple-element.24), channel_id=1, source_target_pairs={{0,1},{1,0},{2,3},{3,2},{4,5},{5,4},{6,7},{7,6},{8,9},{9,8},{10,11... | collective-permute-start | bytes 3145736 | tf_op jit(solution)/shard_map/ppermute | solution.py:222
  43.9 0.1 collective-permute-start.5
  44.0 0.4 collective-permute-start.3
  44.4 0.1 collective-permute-start
  44.5 1.7 %collective-permute-done.1 = f32[2048,128]{1,0:T(8,128)S(1)} collective-permute-done((f32[2048,128]{1,0:T(8,128)S(1)}, f32[2048,128]{1,0:T(8,128)S(1)}, u32[]{:S(2)}, u32[]{:S(2)}) %collective-permute-start.1) | collective-permute-done | bytes 1048608 | tf_op jit(solution)/shard_map/ppermute | solution.py:222
  46.2 0.1 add.94
  46.3 1.4 collective-permute-start.2
  47.7 0.0 collective-permute-done.5
  47.7 0.1 add.97
  47.8 2.8 %collective-permute-start.6 = (f32[2048,128]{1,0:T(8,128)S(1)}, f32[2048,128]{1,0:T(8,128)S(1)}, u32[]{:S(2)}, u32[]{:S(2)}) collective-permute-start(f32[2048,128]{1,0:T(8,128)S(1)} %add.97), channel_id=1, source_target_pairs={{0,6},{1,7},{2,0},{3,1},{4,2},{5,3},{6,4},{7,5},{8,14},{9,15},{10,... | collective-permute-start | bytes 3145736 | tf_op jit(solution)/shard_map/ppermute | solution.py:225
  50.6 0.0 collective-permute-done.3
  50.6 0.1 add.96
  50.7 1.6 %collective-permute-start.4 = (f32[2048,128]{1,0:T(8,128)S(1)}, f32[2048,128]{1,0:T(8,128)S(1)}, u32[]{:S(2)}, u32[]{:S(2)}) collective-permute-start(f32[2048,128]{1,0:T(8,128)S(1)} %add.96), channel_id=1, source_target_pairs={{0,4},{1,5},{2,6},{3,7},{4,0},{5,1},{6,2},{7,3},{8,12},{9,13},{10,... | collective-permute-start | bytes 3145736 | tf_op jit(solution)/shard_map/ppermute | solution.py:225
  52.3 1.4 collective-permute-start.7
  53.7 9.6 %collective-permute-done.7 = bf16[8,64,128]{2,1,0:T(8,128)(2,1)S(1)} collective-permute-done((bf16[8,64,128]{2,1,0:T(8,128)(2,1)S(1)}, bf16[8,64,128]{2,1,0:T(8,128)(2,1)S(1)}, u32[]{:S(2)}, u32[]{:S(2)}) %collective-permute-start.7) | collective-permute-done | bytes 131104 | tf_op jit(solution)/shard_map/ppermute | solution.py:217
  63.3 0.1 collective-permute-start.8
  63.4 9.5 %collective-permute-done.8 = bf16[8,64,128]{2,1,0:T(8,128)(2,1)S(1)} collective-permute-done((bf16[8,64,128]{2,1,0:T(8,128)(2,1)S(1)}, bf16[8,64,128]{2,1,0:T(8,128)(2,1)S(1)}, u32[]{:S(2)}, u32[]{:S(2)}) %collective-permute-start.8) | collective-permute-done | bytes 131104 | tf_op jit(solution)/shard_map/ppermute | solution.py:217
  72.9 0.0 collective-permute-start.9
  72.9 4.4 %collective-permute-done.9 = bf16[8,64,128]{2,1,0:T(8,128)(2,1)S(1)} collective-permute-done((bf16[8,64,128]{2,1,0:T(8,128)(2,1)S(1)}, bf16[8,64,128]{2,1,0:T(8,128)(2,1)S(1)}, u32[]{:S(2)}, u32[]{:S(2)}) %collective-permute-start.9) | collective-permute-done | bytes 131104 | tf_op jit(solution)/shard_map/ppermute | solution.py:217
  77.3 0.9 pad_maximum_fusion
  78.1 0.0 collective-permute-done
  78.1 0.0 collective-permute-done.2
  78.1 17.0 %collective-permute-done.6 = f32[2048,128]{1,0:T(8,128)S(1)} collective-permute-done((f32[2048,128]{1,0:T(8,128)S(1)}, f32[2048,128]{1,0:T(8,128)S(1)}, u32[]{:S(2)}, u32[]{:S(2)}) %collective-permute-start.6) | collective-permute-done | bytes 1048608 | tf_op jit(solution)/shard_map/ppermute | solution.py:225
  95.1 0.7 collective-permute-done.4
  95.8 0.4 add_add_fusion.base_ref
  96.2 26.8 %all-to-all-done.1.recv_ref = bf16[32,64,1024]{2,1,0:T(8,128)(2,1)} async-done(((bf16[32,64,1024]{2,1,0:T(8,128)(2,1)}), bf16[32,64,1024]{2,1,0:T(8,128)(2,1)}, u32[]{:S(2)}, u32[]{:S(2)}) %all-to-all-start.1) | async-done | bytes 4194336 | tf_op jit(solution)/shard_map/all_to_all | solution.py:208
  123.0 3.5 %all-to-all-start.2 = ((bf16[8,4,64,128]{3,2,1,0:T(8,128)(2,1)}), bf16[8,4,64,128]{3,2,1,0:T(8,128)(2,1)S(1)}, u32[]{:S(2)}, u32[]{:S(2)}) async-start(bf16[8,4,64,128]{3,2,1,0:T(8,128)(2,1)} %pad_maximum_fusion), calls=%async_computation.2 | async-start | bytes 1048576 | tf_op jit(solution)/shard_map/all_to_all | solution.py:230
  126.5 5.2 %shard_map.59 = (f32[8,64,128]{2,1,0:T(8,128)S(1)}, f32[8,64,128]{2,1,0:T(8,128)S(1)}) custom-call(s32[2]{0:T(128)S(1)} %pad_add_fusion.place_ref, s32[16]{0:T(128)S(1)} %get-tuple-element.36.owner_ref, bf16[16,128,1024]{2,1,0:T(8,128)(2,1)} %bitcast.37, bf16[32,64,1024]{2,1,0:T(8,128)(2,1)} %all-to-all-done.1.recv_ref), custom_call_target="tpu_custom_call" | custom-call | tf_op jit(solution)/shard_map/pallas_call | solution.py:135
  131.8 4.4 %collective-permute-start.10 = (f32[8,64,128]{2,1,0:T(8,128)S(1)}, f32[8,64,128]{2,1,0:T(8,128)S(1)}, u32[]{:S(2)}, u32[]{:S(2)}) collective-permute-start(f32[8,64,128]{2,1,0:T(8,128)S(1)} %get-tuple-element.32), channel_id=1, source_target_pairs={{0,1},{1,0},{2,3},{3,2},{4,5},{5,4},{6,7},{7,6},{8,9},{9,8},{10,11... | collective-permute-start | bytes 786440 | tf_op jit(solution)/shard_map/ppermute | solution.py:235
  136.1 1.2 collective-permute-done.10
  137.3 11.2 %all-gather = bf16[32,64,128]{2,1,0:T(8,128)(2,1)S(1)} all-gather(bf16[8,64,128]{2,1,0:T(8,128)(2,1)S(1)} %add_convert_fusion), channel_id=2, replica_groups={{0,2,4,6},{1,3,5,7},{8,10,12,14},{9,11,13,15},{16,18,20,22},{17,19,21,2..., dimensions={0}, use_global_device_ids=true | all-gather | bytes 655360 | tf_op jit(solution)/shard_map/all_gather | solution.py:236
  148.6 0.1 reduce_sum.12.mine_ref
  148.6 2.7 %collective-permute-start.11 = (bf16[8,64,128]{2,1,0:T(8,128)(2,1)S(1)}, bf16[8,64,128]{2,1,0:T(8,128)(2,1)S(1)}, u32[]{:S(2)}, u32[]{:S(2)}) collective-permute-start(bf16[8,64,128]{2,1,0:T(8,128)(2,1)S(1)} %reduce_sum.12.mine_ref), channel_id=1, source_target_pairs={{0,1},{1,0},{2,3},{3,2},{4,5},{5,4},{6,7},{7,6},{8,9},{9,8},{10,11... | collective-permute-start | bytes 393224 | tf_op jit(solution)/shard_map/ppermute | solution.py:238
  151.3 1.0 collective-permute-done.11.other_ref
  152.3 1.8 %shard_map.60 = bf16[2048,128]{1,0:T(8,128)(2,1)} custom-call(s32[2]{0:T(128)S(1)} %pad_add_fusion.place_ref, s32[16]{0:T(128)S(1)} %get-tuple-element.35.owner_ref, bf16[8,64,128]{2,1,0:T(8,128)(2,1)S(1)} %reduce_sum.12.mine_ref, bf16[8,64,128]{2,1,0:T(8,128)(2,1)S(1)} %collective-permute-done.11.other_ref, bf16[32,64,128]{2,1,0:T(8,128)(2,1)S(1)} %bitcast.39, ...), custom_call_target="tpu_custom_call" | custom-call | tf_op jit(solution)/shard_map/pallas_call | solution.py:168
  (12 shorter events, 0.1 us)
Async XLA Ops:
  0.0 0.7 copy-start.3
  25.2 5.7 %copy-start.2 = (bf16[32,64,128]{2,1,0:T(8,128)(2,1)S(1)}, bf16[32,64,128]{2,1,0:T(8,128)(2,1)}, u32[]{:S(2)}) copy-start(bf16[32,64,128]{2,1,0:T(8,128)(2,1)} %src_ref.1) | copy-start | bytes 1572868
  25.2 7.3 %copy-start.1 = (bf16[1024,1024]{1,0:T(8,128)(2,1)S(1)}, bf16[1024,1024]{1,0:T(8,128)(2,1)}, u32[]{:S(2)}) copy-start(bf16[1024,1024]{1,0:T(8,128)(2,1)} %wgt_ref.1) | copy-start | bytes 6291460
  25.3 97.7 %all-to-all-start.1 = ((bf16[32,64,1024]{2,1,0:T(8,128)(2,1)}), bf16[32,64,1024]{2,1,0:T(8,128)(2,1)}, u32[]{:S(2)}, u32[]{:S(2)}) async-start(bf16[32,64,1024]{2,1,0:T(8,128)(2,1)} %shard_map.57), calls=%async_computation.1 | async-start | bytes 8388608 | tf_op jit(solution)/shard_map/all_to_all | solution.py:208
  32.6 2.2 %copy-start = (bf16[2048,1024]{1,0:T(8,128)(2,1)S(1)}, bf16[2048,1024]{1,0:T(8,128)(2,1)}, u32[]{:S(2)}) copy-start(bf16[2048,1024]{1,0:T(8,128)(2,1)} %tok_ref) | copy-start | bytes 12582916
  41.7 4.5 %collective-permute-start.1 = (f32[2048,128]{1,0:T(8,128)S(1)}, f32[2048,128]{1,0:T(8,128)S(1)}, u32[]{:S(2)}, u32[]{:S(2)}) collective-permute-start(f32[2048,128]{1,0:T(8,128)S(1)} %get-tuple-element.24), channel_id=1, source_target_pairs={{0,1},{1,0},{2,3},{3,2},{4,5},{5,4},{6,7},{7,6},{8,9},{9,8},{10,11... | collective-permute-start | bytes 3145736 | tf_op jit(solution)/shard_map/ppermute | solution.py:222
  43.9 3.8 %collective-permute-start.5 = (f32[2048,128]{1,0:T(8,128)S(1)}, f32[2048,128]{1,0:T(8,128)S(1)}, u32[]{:S(2)}, u32[]{:S(2)}) collective-permute-start(f32[2048,128]{1,0:T(8,128)S(1)} %get-tuple-element.28), channel_id=1, source_target_pairs={{0,1},{1,0},{2,3},{3,2},{4,5},{5,4},{6,7},{7,6},{8,9},{9,8},{10,11... | collective-permute-start | bytes 3145736 | tf_op jit(solution)/shard_map/ppermute | solution.py:222
  44.0 6.6 %collective-permute-start.3 = (f32[2048,128]{1,0:T(8,128)S(1)}, f32[2048,128]{1,0:T(8,128)S(1)}, u32[]{:S(2)}, u32[]{:S(2)}) collective-permute-start(f32[2048,128]{1,0:T(8,128)S(1)} %get-tuple-element.26), channel_id=1, source_target_pairs={{0,1},{1,0},{2,3},{3,2},{4,5},{5,4},{6,7},{7,6},{8,9},{9,8},{10,11... | collective-permute-start | bytes 3145736 | tf_op jit(solution)/shard_map/ppermute | solution.py:222
  44.4 33.7 %collective-permute-start = (f32[2048,128]{1,0:T(8,128)S(1)}, f32[2048,128]{1,0:T(8,128)S(1)}, u32[]{:S(2)}, u32[]{:S(2)}) collective-permute-start(f32[2048,128]{1,0:T(8,128)S(1)} %get-tuple-element.22), channel_id=1, source_target_pairs={{0,1},{1,0},{2,3},{3,2},{4,5},{5,4},{6,7},{7,6},{8,9},{9,8},{10,11... | collective-permute-start | bytes 3145736 | tf_op jit(solution)/shard_map/ppermute | solution.py:222
  46.3 31.9 %collective-permute-start.2 = (f32[2048,128]{1,0:T(8,128)S(1)}, f32[2048,128]{1,0:T(8,128)S(1)}, u32[]{:S(2)}, u32[]{:S(2)}) collective-permute-start(f32[2048,128]{1,0:T(8,128)S(1)} %add.94), channel_id=1, source_target_pairs={{0,2},{1,3},{2,4},{3,5},{4,6},{5,7},{6,0},{7,1},{8,10},{9,11},{10,... | collective-permute-start | bytes 3145736 | tf_op jit(solution)/shard_map/ppermute | solution.py:225
  47.8 47.3 %collective-permute-start.6 = (f32[2048,128]{1,0:T(8,128)S(1)}, f32[2048,128]{1,0:T(8,128)S(1)}, u32[]{:S(2)}, u32[]{:S(2)}) collective-permute-start(f32[2048,128]{1,0:T(8,128)S(1)} %add.97), channel_id=1, source_target_pairs={{0,6},{1,7},{2,0},{3,1},{4,2},{5,3},{6,4},{7,5},{8,14},{9,15},{10,... | collective-permute-start | bytes 3145736 | tf_op jit(solution)/shard_map/ppermute | solution.py:225
  50.7 45.1 %collective-permute-start.4 = (f32[2048,128]{1,0:T(8,128)S(1)}, f32[2048,128]{1,0:T(8,128)S(1)}, u32[]{:S(2)}, u32[]{:S(2)}) collective-permute-start(f32[2048,128]{1,0:T(8,128)S(1)} %add.96), channel_id=1, source_target_pairs={{0,4},{1,5},{2,6},{3,7},{4,0},{5,1},{6,2},{7,3},{8,12},{9,13},{10,... | collective-permute-start | bytes 3145736 | tf_op jit(solution)/shard_map/ppermute | solution.py:225
  52.3 11.0 %collective-permute-start.7 = (bf16[8,64,128]{2,1,0:T(8,128)(2,1)S(1)}, bf16[8,64,128]{2,1,0:T(8,128)(2,1)S(1)}, u32[]{:S(2)}, u32[]{:S(2)}) collective-permute-start(bf16[8,64,128]{2,1,0:T(8,128)(2,1)S(1)} %get-tuple-element.40), channel_id=1, source_target_pairs={{0,8},{8,16},{16,24},{24,0},{32,40},{40,48},{48,56},{56,32},{64,72... | collective-permute-start | bytes 393224 | tf_op jit(solution)/shard_map/ppermute | solution.py:217
  63.3 9.6 %collective-permute-start.8 = (bf16[8,64,128]{2,1,0:T(8,128)(2,1)S(1)}, bf16[8,64,128]{2,1,0:T(8,128)(2,1)S(1)}, u32[]{:S(2)}, u32[]{:S(2)}) collective-permute-start(bf16[8,64,128]{2,1,0:T(8,128)(2,1)S(1)} %get-tuple-element.39), channel_id=1, source_target_pairs={{0,16},{8,24},{16,0},{24,8},{32,48},{40,56},{48,32},{56,40},{64,80... | collective-permute-start | bytes 393224 | tf_op jit(solution)/shard_map/ppermute | solution.py:217
  72.9 4.4 %collective-permute-start.9 = (bf16[8,64,128]{2,1,0:T(8,128)(2,1)S(1)}, bf16[8,64,128]{2,1,0:T(8,128)(2,1)S(1)}, u32[]{:S(2)}, u32[]{:S(2)}) collective-permute-start(bf16[8,64,128]{2,1,0:T(8,128)(2,1)S(1)} %get-tuple-element.38), channel_id=1, source_target_pairs={{0,24},{8,0},{16,8},{24,16},{32,56},{40,32},{48,40},{56,48},{64,88... | collective-permute-start | bytes 393224 | tf_op jit(solution)/shard_map/ppermute | solution.py:217
  77.3 49.2 %copy-start.4 = (s32[1,16]{1,0:T(1,128)S(1)}, s32[1,16]{1,0:T(1,128)}, u32[]{:S(2)}) copy-start(s32[1,16]{1,0:T(1,128)} %table_ref.1) | copy-start | bytes 196
  123.0 29.3 %all-to-all-start.2 = ((bf16[8,4,64,128]{3,2,1,0:T(8,128)(2,1)}), bf16[8,4,64,128]{3,2,1,0:T(8,128)(2,1)S(1)}, u32[]{:S(2)}, u32[]{:S(2)}) async-start(bf16[8,4,64,128]{3,2,1,0:T(8,128)(2,1)} %pad_maximum_fusion), calls=%async_computation.2 | async-start | bytes 1048576 | tf_op jit(solution)/shard_map/all_to_all | solution.py:230
  131.8 5.5 %collective-permute-start.10 = (f32[8,64,128]{2,1,0:T(8,128)S(1)}, f32[8,64,128]{2,1,0:T(8,128)S(1)}, u32[]{:S(2)}, u32[]{:S(2)}) collective-permute-start(f32[8,64,128]{2,1,0:T(8,128)S(1)} %get-tuple-element.32), channel_id=1, source_target_pairs={{0,1},{1,0},{2,3},{3,2},{4,5},{5,4},{6,7},{7,6},{8,9},{9,8},{10,11... | collective-permute-start | bytes 786440 | tf_op jit(solution)/shard_map/ppermute | solution.py:235
  148.6 3.7 %collective-permute-start.11 = (bf16[8,64,128]{2,1,0:T(8,128)(2,1)S(1)}, bf16[8,64,128]{2,1,0:T(8,128)(2,1)S(1)}, u32[]{:S(2)}, u32[]{:S(2)}) collective-permute-start(bf16[8,64,128]{2,1,0:T(8,128)(2,1)S(1)} %reduce_sum.12.mine_ref), channel_id=1, source_target_pairs={{0,1},{1,0},{2,3},{3,2},{4,5},{5,4},{6,7},{7,6},{8,9},{9,8},{10,11... | collective-permute-start | bytes 393224 | tf_op jit(solution)/shard_map/ppermute | solution.py:238

commit v7 on v5

--- a/solution.py
+++ b/solution.py
@@ -198,12 +198,13 @@
     base = (sums[0] + sums[1]) + (sums[2] + sums[3])
 
     received, base, outgoing_up = lax.optimization_barrier((received, base, outgoing_up))
+    up_slot = owner - owner % lines + (my_line - owner % lines) % lines
+    keep, give = down_products(place, owner, tokens.reshape(blocks, BLOCK, feat_dev), received)
+    keep, give, outgoing_up = lax.optimization_barrier((keep, give, outgoing_up))
     columns_z = [[z * lines + x for z in range(layers)] for x in range(lines)]
     ups = lax.all_to_all(
         outgoing_up, "dp", split_axis=0, concat_axis=0, tiled=True, axis_index_groups=columns_z
     ).reshape((groups,) + adapter_up_factors.shape[1:])
-    up_slot = owner - owner % lines + (my_line - owner % lines) % lines
-    keep, give = down_products(place, owner, tokens.reshape(blocks, BLOCK, feat_dev), received)
     part = (keep + lax.ppermute(give, "tensor", swap)).astype(jnp.bfloat16)
     parts = lax.all_gather(part, "tensor", axis=0, axis_index_groups=columns)
     mine = jnp.sum(parts.astype(jnp.float32), axis=0).astype(jnp.bfloat16)

time: 155 us -> 154 us (level)
  transfers between devices with their start and end apart: 14 -> 14, of which waited for: 9 -> 9; matrix products, arithmetic and copies ran while one was open for 2% -> 2% of each run, Pallas kernels for 9% -> 6%
where the time goes in v7:
time: 154 us
  waiting for transfers between devices  66.7 us (43%)
  blocking collectives  31.7 us (21%)
  starting transfers between devices  29.3 us (19%)
  Pallas kernels  19.8 us (13%)
  other arithmetic  3.23 us (2%)
  local copies, waits for them, and re-layouts  3.14 us (2%)
    all_to_all x1, waiting for transfers between devices, local(): lax.all_to_all(outgoing, 'dp', split_axis=0, concat_axis=0, tiled=True)  25.9 us
    all_to_all x1, blocking collectives, local(): lax.all_to_all(asked[:, None], 'dp', split_axis=0, concat_axis=0, tiled=T...  20.2 us
    ppermute x3, waiting for transfers between devices, local(): sums[k] = lax.ppermute(sums[k], 'tensor', along)  20.1 us
    ppermute x3, waiting for transfers between devices, local(): moved.append(lax.ppermute(up_lines[d], 'dp', along))  16.8 us
    all_gather x1, blocking collectives, local(): parts = lax.all_gather(part, 'tensor', axis=0, axis_index_groups=columns)  11.5 us
    pallas_call x1, Pallas kernels, base_products(): pl.pallas_call(base_kernel, out_shape=tuple((jax.ShapeDtypeStruct((rows,...  6.9 us
    pallas_call x2, Pallas kernels, pick(): pl.pallas_call(pick_kernel, out_shape=jax.ShapeDtypeStruct(src.shape, src...  5.8 us
    ppermute x3, starting transfers between devices, local(): sums[k] = lax.ppermute(sums[k], 'tensor', along)  5.76 us
  transfers between devices with their start and end apart: 14, of which 9 were waited for; matrix products, arithmetic and copies ran while one was open for 2% of the time, Pallas kernels for 6%

profile of v7, /device:TPU:1, one launch (start us, length us, event | category | flops | bytes accessed | tf_op | source)
XLA Modules:
  0.0 154.0 jit_solution(15497921735826760817)
XLA Ops:
  0.0 0.7 subtract_bitcast_fusion
  0.7 0.1 select_reduce_fusion
  0.8 0.1 copy.32
  0.8 20.2 %all_to_all.21 = s32[32,1,1]{2,1,0:T(1,128)S(1)} all-to-all(s32[32,1,1]{2,1,0:T(1,128)S(1)} %copy.32), channel_id=1, replica_groups=mesh['dp'=32,'tensor'=8] {'dp'}, dimensions={0} | all-to-all | bytes 256 | tf_op jit(solution)/shard_map/all_to_all | solution.py:175
  21.1 4.2 %shard_map.56 = bf16[32,64,1024]{2,1,0:T(8,128)(2,1)} custom-call(s32[32,1]{1,0:T(8,128)S(1)} %bitcast.43, bf16[32,64,1024]{2,1,0:T(8,128)(2,1)} %bitcast.44), custom_call_target="tpu_custom_call" | custom-call | tf_op jit(solution)/shard_map/pallas_call | solution.py:29
  25.3 0.0 copy-start.2
  25.3 5.0 %all-to-all-start.1 = ((bf16[32,64,1024]{2,1,0:T(8,128)(2,1)}), bf16[32,64,1024]{2,1,0:T(8,128)(2,1)}, u32[]{:S(2)}, u32[]{:S(2)}) async-start(bf16[32,64,1024]{2,1,0:T(8,128)(2,1)} %shard_map.56), calls=%async_computation.1 | async-start | bytes 8388608 | tf_op jit(solution)/shard_map/all_to_all | solution.py:181
  30.4 0.1 pad_add_fusion.place_ref
  30.5 0.7 reduce.1
  31.1 0.1 reshape.68
  31.2 0.1 copy.33
  31.3 0.6 gather_fusion
  31.8 0.1 reshape.82.ids_ref
  31.9 1.6 %shard_map.55 = bf16[32,64,128]{2,1,0:T(8,128)(2,1)S(1)} custom-call(s32[32,1]{1,0:T(8,128)S(1)} %reshape.82.ids_ref, bf16[32,64,128]{2,1,0:T(8,128)(2,1)S(1)} %copy-done.2), custom_call_target="tpu_custom_call" | custom-call | tf_op jit(solution)/shard_map/pallas_call | solution.py:29
  33.6 0.0 copy-start
  33.6 2.2 %copy-done = bf16[2048,1024]{1,0:T(8,128)(2,1)S(1)} copy-done((bf16[2048,1024]{1,0:T(8,128)(2,1)S(1)}, bf16[2048,1024]{1,0:T(8,128)(2,1)}, u32[]{:S(2)}) %copy-start) | copy-done | bytes 4194328
  35.7 6.9 %shard_map.57 = (f32[2048,128]{1,0:T(8,128)S(1)}, f32[2048,128]{1,0:T(8,128)S(1)}, f32[2048,128]{1,0:T(8,128)S(1)}, f32[2048,128]{1,0:T(8,128)S(1)}, f32[2048,12...) custom-call(s32[2]{0:T(128)S(1)} %pad_add_fusion.place_ref, ...), custom_call_target="tpu_custom_call" | custom-call | tf_op jit(solution)/shard_map/pallas_call | solution.py:62
  42.7 2.2 %collective-permute-start.1 = (f32[2048,128]{1,0:T(8,128)S(1)}, f32[2048,128]{1,0:T(8,128)S(1)}, u32[]{:S(2)}, u32[]{:S(2)}) collective-permute-start(f32[2048,128]{1,0:T(8,128)S(1)} %get-tuple-element.27), channel_id=1, source_target_pairs={{0,1},{1,0},{2,3},{3,2},{4,5},{5,4},{6,7},{7,6},{8,9},{9,8},{10,11... | collective-permute-start | bytes 3145736 | tf_op jit(solution)/shard_map/ppermute | solution.py:194
  44.9 0.1 collective-permute-start.5
  45.0 0.4 collective-permute-start.3
  45.4 0.1 collective-permute-start
  45.5 1.7 %collective-permute-done.1 = f32[2048,128]{1,0:T(8,128)S(1)} collective-permute-done((f32[2048,128]{1,0:T(8,128)S(1)}, f32[2048,128]{1,0:T(8,128)S(1)}, u32[]{:S(2)}, u32[]{:S(2)}) %collective-permute-start.1) | collective-permute-done | bytes 1048608 | tf_op jit(solution)/shard_map/ppermute | solution.py:194
  47.1 0.1 add.96
  47.3 1.4 collective-permute-start.2
  48.6 0.1 add.99
  48.8 2.8 %collective-permute-start.6 = (f32[2048,128]{1,0:T(8,128)S(1)}, f32[2048,128]{1,0:T(8,128)S(1)}, u32[]{:S(2)}, u32[]{:S(2)}) collective-permute-start(f32[2048,128]{1,0:T(8,128)S(1)} %add.99), channel_id=1, source_target_pairs={{0,6},{1,7},{2,0},{3,1},{4,2},{5,3},{6,4},{7,5},{8,14},{9,15},{10,... | collective-permute-start | bytes 3145736 | tf_op jit(solution)/shard_map/ppermute | solution.py:197
  51.6 0.1 add.98
  51.7 1.6 %collective-permute-start.4 = (f32[2048,128]{1,0:T(8,128)S(1)}, f32[2048,128]{1,0:T(8,128)S(1)}, u32[]{:S(2)}, u32[]{:S(2)}) collective-permute-start(f32[2048,128]{1,0:T(8,128)S(1)} %add.98), channel_id=1, source_target_pairs={{0,4},{1,5},{2,6},{3,7},{4,0},{5,1},{6,2},{7,3},{8,12},{9,13},{10,... | collective-permute-start | bytes 3145736 | tf_op jit(solution)/shard_map/ppermute | solution.py:197
  53.3 1.4 collective-permute-start.7
  54.7 7.6 %collective-permute-done.7 = bf16[8,64,128]{2,1,0:T(8,128)(2,1)S(1)} collective-permute-done((bf16[8,64,128]{2,1,0:T(8,128)(2,1)S(1)}, bf16[8,64,128]{2,1,0:T(8,128)(2,1)S(1)}, u32[]{:S(2)}, u32[]{:S(2)}) %collective-permute-start.7) | collective-permute-done | bytes 131104 | tf_op jit(solution)/shard_map/ppermute | solution.py:189
  62.2 3.9 %collective-permute-start.8 = (bf16[8,64,128]{2,1,0:T(8,128)(2,1)S(1)}, bf16[8,64,128]{2,1,0:T(8,128)(2,1)S(1)}, u32[]{:S(2)}, u32[]{:S(2)}) collective-permute-start(bf16[8,64,128]{2,1,0:T(8,128)(2,1)S(1)} %get-tuple-element.47), channel_id=1, source_target_pairs={{0,16},{8,24},{16,0},{24,8},{32,48},{40,56},{48,32},{56,40},{64,80... | collective-permute-start | bytes 393224 | tf_op jit(solution)/shard_map/ppermute | solution.py:189
  66.1 5.1 %collective-permute-done.8 = bf16[8,64,128]{2,1,0:T(8,128)(2,1)S(1)} collective-permute-done((bf16[8,64,128]{2,1,0:T(8,128)(2,1)S(1)}, bf16[8,64,128]{2,1,0:T(8,128)(2,1)S(1)}, u32[]{:S(2)}, u32[]{:S(2)}) %collective-permute-start.8) | collective-permute-done | bytes 131104 | tf_op jit(solution)/shard_map/ppermute | solution.py:189
  71.2 0.4 collective-permute-start.9
  71.6 4.1 %collective-permute-done.9 = bf16[8,64,128]{2,1,0:T(8,128)(2,1)S(1)} collective-permute-done((bf16[8,64,128]{2,1,0:T(8,128)(2,1)S(1)}, bf16[8,64,128]{2,1,0:T(8,128)(2,1)S(1)}, u32[]{:S(2)}, u32[]{:S(2)}) %collective-permute-start.9) | collective-permute-done | bytes 131104 | tf_op jit(solution)/shard_map/ppermute | solution.py:189
  75.7 0.9 pad_maximum_fusion
  76.6 19.5 %collective-permute-done.6 = f32[2048,128]{1,0:T(8,128)S(1)} collective-permute-done((f32[2048,128]{1,0:T(8,128)S(1)}, f32[2048,128]{1,0:T(8,128)S(1)}, u32[]{:S(2)}, u32[]{:S(2)}) %collective-permute-start.6) | collective-permute-done | bytes 1048608 | tf_op jit(solution)/shard_map/ppermute | solution.py:197
  96.1 0.7 collective-permute-done.4
  96.7 0.4 add_add_fusion.base_ref
  97.1 25.9 %all-to-all-done.1.recv_ref = bf16[32,64,1024]{2,1,0:T(8,128)(2,1)} async-done(((bf16[32,64,1024]{2,1,0:T(8,128)(2,1)}), bf16[32,64,1024]{2,1,0:T(8,128)(2,1)}, u32[]{:S(2)}, u32[]{:S(2)}) %all-to-all-start.1) | async-done | bytes 4194336 | tf_op jit(solution)/shard_map/all_to_all | solution.py:181
  123.1 5.3 %shard_map.58 = (f32[8,64,128]{2,1,0:T(8,128)S(1)}, f32[8,64,128]{2,1,0:T(8,128)S(1)}) custom-call(s32[2]{0:T(128)S(1)} %pad_add_fusion.place_ref, s32[16]{0:T(128)S(1)} %get-tuple-element.44.owner_ref, bf16[16,128,1024]{2,1,0:T(8,128)(2,1)} %bitcast.40, bf16[32,64,1024]{2,1,0:T(8,128)(2,1)} %all-to-all-done.1.recv_ref), custom_call_target="tpu_custom_call" | custom-call | tf_op jit(solution)/shard_map/pallas_call | solution.py:107
  128.3 3.5 %all-to-all-start.2 = ((bf16[8,4,64,128]{3,2,1,0:T(8,128)(2,1)}), bf16[8,4,64,128]{3,2,1,0:T(8,128)(2,1)S(1)}, u32[]{:S(2)}, u32[]{:S(2)}) async-start(bf16[8,4,64,128]{3,2,1,0:T(8,128)(2,1)} %pad_maximum_fusion), calls=%async_computation.2 | async-start | bytes 1048576 | tf_op jit(solution)/shard_map/all_to_all | solution.py:205
  131.9 4.3 %collective-permute-start.10 = (f32[8,64,128]{2,1,0:T(8,128)S(1)}, f32[8,64,128]{2,1,0:T(8,128)S(1)}, u32[]{:S(2)}, u32[]{:S(2)}) collective-permute-start(f32[8,64,128]{2,1,0:T(8,128)S(1)} %get-tuple-element.38), channel_id=1, source_target_pairs={{0,1},{1,0},{2,3},{3,2},{4,5},{5,4},{6,7},{7,6},{8,9},{9,8},{10,11... | collective-permute-start | bytes 786440 | tf_op jit(solution)/shard_map/ppermute | solution.py:208
  136.2 1.2 collective-permute-done.10
  137.4 11.5 %all-gather = bf16[32,64,128]{2,1,0:T(8,128)(2,1)S(1)} all-gather(bf16[8,64,128]{2,1,0:T(8,128)(2,1)S(1)} %add_convert_fusion), channel_id=2, replica_groups={{0,2,4,6},{1,3,5,7},{8,10,12,14},{9,11,13,15},{16,18,20,22},{17,19,21,2..., dimensions={0}, use_global_device_ids=true | all-gather | bytes 655360 | tf_op jit(solution)/shard_map/all_gather | solution.py:209
  148.9 0.1 reduce_sum.22.mine_ref
  148.9 2.3 %collective-permute-start.11 = (bf16[8,64,128]{2,1,0:T(8,128)(2,1)S(1)}, bf16[8,64,128]{2,1,0:T(8,128)(2,1)S(1)}, u32[]{:S(2)}, u32[]{:S(2)}) collective-permute-start(bf16[8,64,128]{2,1,0:T(8,128)(2,1)S(1)} %reduce_sum.22.mine_ref), channel_id=1, source_target_pairs={{0,1},{1,0},{2,3},{3,2},{4,5},{5,4},{6,7},{7,6},{8,9},{9,8},{10,11... | collective-permute-start | bytes 393224 | tf_op jit(solution)/shard_map/ppermute | solution.py:211
  151.2 1.0 collective-permute-done.11.other_ref
  152.2 1.8 %shard_map.59 = bf16[2048,128]{1,0:T(8,128)(2,1)} custom-call(s32[2]{0:T(128)S(1)} %pad_add_fusion.place_ref, s32[16]{0:T(128)S(1)} %get-tuple-element.43.owner_ref, bf16[8,64,128]{2,1,0:T(8,128)(2,1)S(1)} %reduce_sum.22.mine_ref, bf16[8,64,128]{2,1,0:T(8,128)(2,1)S(1)} %collective-permute-done.11.other_ref, bf16[32,64,128]{2,1,0:T(8,128)(2,1)S(1)} %bitcast.42, ...), custom_call_target="tpu_custom_call" | custom-call | tf_op jit(solution)/shard_map/pallas_call | solution.py:140
  (15 shorter events, 0.1 us)
Async XLA Ops:
  25.3 6.6 %copy-start.2 = (bf16[32,64,128]{2,1,0:T(8,128)(2,1)S(1)}, bf16[32,64,128]{2,1,0:T(8,128)(2,1)}, u32[]{:S(2)}) copy-start(bf16[32,64,128]{2,1,0:T(8,128)(2,1)} %src_ref.1) | copy-start | bytes 1572868
  25.3 8.3 %copy-start.1 = (bf16[1024,1024]{1,0:T(8,128)(2,1)S(1)}, bf16[1024,1024]{1,0:T(8,128)(2,1)}, u32[]{:S(2)}) copy-start(bf16[1024,1024]{1,0:T(8,128)(2,1)} %wgt_ref.1) | copy-start | bytes 6291460
  25.3 97.7 %all-to-all-start.1 = ((bf16[32,64,1024]{2,1,0:T(8,128)(2,1)}), bf16[32,64,1024]{2,1,0:T(8,128)(2,1)}, u32[]{:S(2)}, u32[]{:S(2)}) async-start(bf16[32,64,1024]{2,1,0:T(8,128)(2,1)} %shard_map.56), calls=%async_computation.1 | async-start | bytes 8388608 | tf_op jit(solution)/shard_map/all_to_all | solution.py:181
  33.6 2.2 %copy-start = (bf16[2048,1024]{1,0:T(8,128)(2,1)S(1)}, bf16[2048,1024]{1,0:T(8,128)(2,1)}, u32[]{:S(2)}) copy-start(bf16[2048,1024]{1,0:T(8,128)(2,1)} %tok_ref) | copy-start | bytes 12582916
  42.7 4.5 %collective-permute-start.1 = (f32[2048,128]{1,0:T(8,128)S(1)}, f32[2048,128]{1,0:T(8,128)S(1)}, u32[]{:S(2)}, u32[]{:S(2)}) collective-permute-start(f32[2048,128]{1,0:T(8,128)S(1)} %get-tuple-element.27), channel_id=1, source_target_pairs={{0,1},{1,0},{2,3},{3,2},{4,5},{5,4},{6,7},{7,6},{8,9},{9,8},{10,11... | collective-permute-start | bytes 3145736 | tf_op jit(solution)/shard_map/ppermute | solution.py:194
  44.9 3.8 %collective-permute-start.5 = (f32[2048,128]{1,0:T(8,128)S(1)}, f32[2048,128]{1,0:T(8,128)S(1)}, u32[]{:S(2)}, u32[]{:S(2)}) collective-permute-start(f32[2048,128]{1,0:T(8,128)S(1)} %get-tuple-element.31), channel_id=1, source_target_pairs={{0,1},{1,0},{2,3},{3,2},{4,5},{5,4},{6,7},{7,6},{8,9},{9,8},{10,11... | collective-permute-start | bytes 3145736 | tf_op jit(solution)/shard_map/ppermute | solution.py:194
  45.0 6.6 %collective-permute-start.3 = (f32[2048,128]{1,0:T(8,128)S(1)}, f32[2048,128]{1,0:T(8,128)S(1)}, u32[]{:S(2)}, u32[]{:S(2)}) collective-permute-start(f32[2048,128]{1,0:T(8,128)S(1)} %get-tuple-element.29), channel_id=1, source_target_pairs={{0,1},{1,0},{2,3},{3,2},{4,5},{5,4},{6,7},{7,6},{8,9},{9,8},{10,11... | collective-permute-start | bytes 3145736 | tf_op jit(solution)/shard_map/ppermute | solution.py:194
  45.4 31.2 %collective-permute-start = (f32[2048,128]{1,0:T(8,128)S(1)}, f32[2048,128]{1,0:T(8,128)S(1)}, u32[]{:S(2)}, u32[]{:S(2)}) collective-permute-start(f32[2048,128]{1,0:T(8,128)S(1)} %get-tuple-element.25), channel_id=1, source_target_pairs={{0,1},{1,0},{2,3},{3,2},{4,5},{5,4},{6,7},{7,6},{8,9},{9,8},{10,11... | collective-permute-start | bytes 3145736 | tf_op jit(solution)/shard_map/ppermute | solution.py:194
  47.2 24.3 %copy-start.3 = (s32[1,16]{1,0:T(1,128)S(1)}, s32[1,16]{1,0:T(1,128)}, u32[]{:S(2)}) copy-start(s32[1,16]{1,0:T(1,128)} %param.9) | copy-start | bytes 196
  47.3 29.3 %collective-permute-start.2 = (f32[2048,128]{1,0:T(8,128)S(1)}, f32[2048,128]{1,0:T(8,128)S(1)}, u32[]{:S(2)}, u32[]{:S(2)}) collective-permute-start(f32[2048,128]{1,0:T(8,128)S(1)} %add.96), channel_id=1, source_target_pairs={{0,2},{1,3},{2,4},{3,5},{4,6},{5,7},{6,0},{7,1},{8,10},{9,11},{10,... | collective-permute-start | bytes 3145736 | tf_op jit(solution)/shard_map/ppermute | solution.py:197
  48.8 47.3 %collective-permute-start.6 = (f32[2048,128]{1,0:T(8,128)S(1)}, f32[2048,128]{1,0:T(8,128)S(1)}, u32[]{:S(2)}, u32[]{:S(2)}) collective-permute-start(f32[2048,128]{1,0:T(8,128)S(1)} %add.99), channel_id=1, source_target_pairs={{0,6},{1,7},{2,0},{3,1},{4,2},{5,3},{6,4},{7,5},{8,14},{9,15},{10,... | collective-permute-start | bytes 3145736 | tf_op jit(solution)/shard_map/ppermute | solution.py:197
  51.7 45.1 %collective-permute-start.4 = (f32[2048,128]{1,0:T(8,128)S(1)}, f32[2048,128]{1,0:T(8,128)S(1)}, u32[]{:S(2)}, u32[]{:S(2)}) collective-permute-start(f32[2048,128]{1,0:T(8,128)S(1)} %add.98), channel_id=1, source_target_pairs={{0,4},{1,5},{2,6},{3,7},{4,0},{5,1},{6,2},{7,3},{8,12},{9,13},{10,... | collective-permute-start | bytes 3145736 | tf_op jit(solution)/shard_map/ppermute | solution.py:197
  53.3 9.0 %collective-permute-start.7 = (bf16[8,64,128]{2,1,0:T(8,128)(2,1)S(1)}, bf16[8,64,128]{2,1,0:T(8,128)(2,1)S(1)}, u32[]{:S(2)}, u32[]{:S(2)}) collective-permute-start(bf16[8,64,128]{2,1,0:T(8,128)(2,1)S(1)} %get-tuple-element.48), channel_id=1, source_target_pairs={{0,8},{8,16},{16,24},{24,0},{32,40},{40,48},{48,56},{56,32},{64,72... | collective-permute-start | bytes 393224 | tf_op jit(solution)/shard_map/ppermute | solution.py:189
  62.2 9.0 %collective-permute-start.8 = (bf16[8,64,128]{2,1,0:T(8,128)(2,1)S(1)}, bf16[8,64,128]{2,1,0:T(8,128)(2,1)S(1)}, u32[]{:S(2)}, u32[]{:S(2)}) collective-permute-start(bf16[8,64,128]{2,1,0:T(8,128)(2,1)S(1)} %get-tuple-element.47), channel_id=1, source_target_pairs={{0,16},{8,24},{16,0},{24,8},{32,48},{40,56},{48,32},{56,40},{64,80... | collective-permute-start | bytes 393224 | tf_op jit(solution)/shard_map/ppermute | solution.py:189
  71.2 4.5 %collective-permute-start.9 = (bf16[8,64,128]{2,1,0:T(8,128)(2,1)S(1)}, bf16[8,64,128]{2,1,0:T(8,128)(2,1)S(1)}, u32[]{:S(2)}, u32[]{:S(2)}) collective-permute-start(bf16[8,64,128]{2,1,0:T(8,128)(2,1)S(1)} %get-tuple-element.46), channel_id=1, source_target_pairs={{0,24},{8,0},{16,8},{24,16},{32,56},{40,32},{48,40},{56,48},{64,88... | collective-permute-start | bytes 393224 | tf_op jit(solution)/shard_map/ppermute | solution.py:189
  128.3 23.8 %all-to-all-start.2 = ((bf16[8,4,64,128]{3,2,1,0:T(8,128)(2,1)}), bf16[8,4,64,128]{3,2,1,0:T(8,128)(2,1)S(1)}, u32[]{:S(2)}, u32[]{:S(2)}) async-start(bf16[8,4,64,128]{3,2,1,0:T(8,128)(2,1)} %pad_maximum_fusion), calls=%async_computation.2 | async-start | bytes 1048576 | tf_op jit(solution)/shard_map/all_to_all | solution.py:205
  131.9 5.5 %collective-permute-start.10 = (f32[8,64,128]{2,1,0:T(8,128)S(1)}, f32[8,64,128]{2,1,0:T(8,128)S(1)}, u32[]{:S(2)}, u32[]{:S(2)}) collective-permute-start(f32[8,64,128]{2,1,0:T(8,128)S(1)} %get-tuple-element.38), channel_id=1, source_target_pairs={{0,1},{1,0},{2,3},{3,2},{4,5},{5,4},{6,7},{7,6},{8,9},{9,8},{10,11... | collective-permute-start | bytes 786440 | tf_op jit(solution)/shard_map/ppermute | solution.py:208
  148.9 3.2 %collective-permute-start.11 = (bf16[8,64,128]{2,1,0:T(8,128)(2,1)S(1)}, bf16[8,64,128]{2,1,0:T(8,128)(2,1)S(1)}, u32[]{:S(2)}, u32[]{:S(2)}) collective-permute-start(bf16[8,64,128]{2,1,0:T(8,128)(2,1)S(1)} %reduce_sum.22.mine_ref), channel_id=1, source_target_pairs={{0,1},{1,0},{2,3},{3,2},{4,5},{5,4},{6,7},{7,6},{8,9},{9,8},{10,11... | collective-permute-start | bytes 393224 | tf_op jit(solution)/shard_map/ppermute | solution.py:211
